TPU v7x, 32 devices: a whole 2x2x4 slice. The times are simulated.
32 devices in a mesh: dp: 8 (over z, x), head: 4 (over y, core).
Axes of the slice: x: 2, y: 2, z: 4, core: 2. Of those that a mesh axis runs over, the one named last changes fastest.
Arguments:
- q_raw: bfloat16 [12288, 2560], P('dp', 'head'), may hold values from -2000 to 2000
- k_raw: bfloat16 [12288, 512], P('dp', 'head'), may hold values from -2000 to 2000
- v_proj: bfloat16 [12288, 512], P('dp', 'head'), may hold values from -6 to 6
- d_out: bfloat16 [12288, 2560], P('dp', 'head'), may hold values from -6 to 6
- q_gain: float32 [2560], P('head'), may hold values from 0.5 to 2
- k_gain: float32 [512], P('head'), may hold values from 0.5 to 2
- doc_lengths: int32 [8, 8], P('dp'), may hold values from 1 to 384, as said below
- plan_dest: int32 [8, 8], P('dp'), may hold values from 0 to 7, as said below
- plan_offset: int32 [8, 8], P('dp'), may hold values from 0 to 192, as said below
Outputs:
- grad_q: bfloat16 [12288, 2560], P('dp', 'head')
- grad_k: bfloat16 [12288, 512], P('dp', 'head')
- grad_v: bfloat16 [12288, 512], P('dp', 'head')
- balanced_lse: float32 [20, 27648], P('head', 'dp')
Inputs may be any that keep to these rules, and one draw needn't show every extreme that they name: `doc_lengths`: each row holds the lengths of one sequence's documents in order and sums to 1536; the largest and the smallest length are reached in every draw. In each row exactly 4 documents have a plan_dest other than the row's own device, no two of them the same device; each of them has 192 to 384 rows, and in every row one has exactly 384 rows and one exactly 192. The documents that keep the row's own device sum to exactly 384 tokens. For a document sent to another device, plan_offset plus its length is at most 384; documents that stay have 0. Every row reaches the largest value.
All inputs are finite; a program needn't handle non-finite values.
Results may differ from a plain program's by a relative error of at most 0.008.
The roundings to bfloat16 on the way count: a program that leaves them out, or rounds other values in their place, can miss the bound.
Values may be sent and summed in bfloat16 or wider, within the bound.
A program may use at most 128 MiB of HBM per device.

v0:
```python
import math

import jax
import jax.numpy as jnp
from jax import lax
from jax.sharding import PartitionSpec as P

HDIM = 128


eps = 1e-06
big_negative = -1e30


def block_backward(q_rows, k_rows, v_rows, grad_rows, tag_q, tag_k, pos_q, pos_k, head_dim):
    rows_q = q_rows.shape[0]
    rows_k = k_rows.shape[0]
    kv_local = k_rows.shape[1] // head_dim
    group_size = q_rows.shape[1] // k_rows.shape[1]
    queries = q_rows.reshape(rows_q, kv_local, group_size, head_dim)
    upstream = grad_rows.reshape(rows_q, kv_local, group_size, head_dim)
    key_heads = k_rows.reshape(rows_k, kv_local, head_dim)
    value_heads = v_rows.reshape(rows_k, kv_local, head_dim)
    scaling = 1.0 / math.sqrt(head_dim)
    allowed = (
        (tag_q[:, None] == tag_k[None, :])
        & (tag_q[:, None] >= 0)
        & (pos_k[None, :] <= pos_q[:, None])
    )
    scores = (
        jnp.einsum("qgjd,kgd->gjqk", queries, key_heads, preferred_element_type=jnp.float32)
        * scaling
    )
    masked = jnp.where(allowed, scores, big_negative)
    row_peak = jnp.max(masked, axis=-1, keepdims=True)
    row_total = jnp.sum(jnp.where(allowed, jnp.exp(masked - row_peak), 0.0), axis=-1, keepdims=True)
    row_live = row_total > 0.0
    log_sums = row_peak + jnp.log(jnp.where(row_live, row_total, 1.0))
    weights = jnp.where(allowed, jnp.exp(masked - log_sums), 0.0)
    weights_low = weights.astype(jnp.bfloat16)
    output = jnp.einsum(
        "gjqk,kgd->qgjd", weights_low, value_heads, preferred_element_type=jnp.float32
    )
    row_delta = jnp.transpose(jnp.sum(upstream.astype(jnp.float32) * output, axis=-1), (1, 2, 0))[
        ..., None
    ]
    grad_values = jnp.einsum(
        "gjqk,qgjd->kgd", weights_low, upstream, preferred_element_type=jnp.float32
    )
    grad_weights = jnp.einsum(
        "qgjd,kgd->gjqk", upstream, value_heads, preferred_element_type=jnp.float32
    )
    grad_low = (weights * (grad_weights - row_delta) * scaling).astype(jnp.bfloat16)
    grad_query = jnp.einsum(
        "gjqk,kgd->qgjd", grad_low, key_heads, preferred_element_type=jnp.float32
    )
    grad_keys = jnp.einsum("gjqk,qgjd->kgd", grad_low, queries, preferred_element_type=jnp.float32)
    log_rows = jnp.where(row_live[..., 0], log_sums[..., 0], 0.0).reshape(
        kv_local * group_size, rows_q
    )
    return (
        grad_query.reshape(rows_q, -1),
        grad_keys.reshape(rows_k, -1),
        grad_values.reshape(rows_k, -1),
        log_rows,
    )


def local(q_raw, k_raw, v_proj, d_out, q_gain, k_gain, doc_lengths, plan_dest, plan_offset):
    head_dim = HDIM
    seq_len = q_raw.shape[0]
    devices = lax.axis_size("dp")
    span = 2 * seq_len
    slot = span // devices
    home_count = seq_len // 4
    width_q = q_raw.shape[1] * lax.axis_size("head")
    width_k = k_raw.shape[1] * lax.axis_size("head")
    q_float = q_raw.astype(jnp.float32)
    k_float = k_raw.astype(jnp.float32)
    sum_q, sum_k = lax.psum(
        (jnp.sum(q_float * q_float, axis=1), jnp.sum(k_float * k_float, axis=1)), "head"
    )
    recip_q = lax.rsqrt(sum_q / width_q + eps)
    recip_k = lax.rsqrt(sum_k / width_k + eps)
    q_norm = (q_float * recip_q[:, None] * q_gain[None, :]).astype(jnp.bfloat16)
    k_norm = (k_float * recip_k[:, None] * k_gain[None, :]).astype(jnp.bfloat16)
    here = lax.axis_index("dp")
    lengths_row = doc_lengths[0]
    ends = jnp.cumsum(lengths_row)
    starts = ends - lengths_row
    row_index = jnp.arange(seq_len, dtype=jnp.int32)
    row_doc = jnp.sum((row_index[:, None] >= ends[None, :]).astype(jnp.int32), axis=1)
    picker = (
        row_doc[:, None] == jnp.arange(lengths_row.shape[0], dtype=jnp.int32)[None, :]
    ).astype(jnp.int32)
    row_dest = jnp.sum(picker * plan_dest[0][None, :], axis=1)
    row_start = jnp.sum(picker * starts[None, :], axis=1)
    row_shift = jnp.sum(picker * plan_offset[0][None, :], axis=1)
    leaving = row_dest != here
    target = jnp.where(leaving, row_dest * slot + row_shift + row_index - row_start, span)
    staying = jnp.logical_not(leaving)
    rank = jnp.cumsum(staying.astype(jnp.int32)) - 1
    home_index = (
        jnp.zeros((home_count,), jnp.int32)
        .at[jnp.where(staying, rank, home_count)]
        .set(row_index, mode="drop")
    )

    def to_slots(rows):
        empty = jnp.zeros((span, rows.shape[1]), rows.dtype)
        return empty.at[target].set(rows, mode="drop").reshape(devices, slot, rows.shape[1])

    present = (
        jnp.zeros((span,), jnp.bfloat16)
        .at[target]
        .set(jnp.ones((seq_len,), jnp.bfloat16), mode="drop")
        .reshape(devices, slot)
    )
    got_q, got_k, got_v, got_grad, got_present = (
        lax.all_to_all(to_slots(q_norm), "dp", split_axis=0, concat_axis=0, tiled=True),
        lax.all_to_all(to_slots(k_norm), "dp", split_axis=0, concat_axis=0, tiled=True),
        lax.all_to_all(to_slots(v_proj), "dp", split_axis=0, concat_axis=0, tiled=True),
        lax.all_to_all(to_slots(d_out), "dp", split_axis=0, concat_axis=0, tiled=True),
        lax.all_to_all(present, "dp", split_axis=0, concat_axis=0, tiled=True),
    )
    home_tags = jnp.take(row_doc, home_index)
    home_q, home_k, home_v, home_log = block_backward(
        jnp.take(q_norm, home_index, axis=0),
        jnp.take(k_norm, home_index, axis=0),
        jnp.take(v_proj, home_index, axis=0),
        jnp.take(d_out, home_index, axis=0),
        home_tags,
        home_tags,
        home_index,
        home_index,
        head_dim,
    )
    span_index = jnp.arange(span, dtype=jnp.int32)
    away_tags = jnp.where(got_present.reshape(span) > 0, span_index // slot, -1)
    per_tile = 1
    while slot * per_tile < 128 and devices % (2 * per_tile) == 0:
        per_tile = per_tile * 2
    tile_rows = slot * per_tile
    tile_count = span // tile_rows
    per_group = 1
    while tile_rows * per_group < 512 and tile_count % (2 * per_group) == 0:
        per_group = per_group * 2
    group_count = tile_count // per_group

    def grouped(values):
        return values.reshape((group_count, per_group, tile_rows) + values.shape[1:])

    def run_tile(q_rows, k_rows, v_rows, g_rows, tags, positions):
        return block_backward(
            q_rows, k_rows, v_rows, g_rows, tags, tags, positions, positions, head_dim
        )

    def tile_group(pieces):
        return jax.vmap(run_tile)(*pieces)

    results = lax.map(
        tile_group,
        (
            grouped(got_q.reshape(span, -1)),
            grouped(got_k.reshape(span, -1)),
            grouped(got_v.reshape(span, -1)),
            grouped(got_grad.reshape(span, -1)),
            grouped(away_tags),
            grouped(span_index),
        ),
    )
    away_q = results[0].reshape(span, -1).astype(jnp.bfloat16).reshape(devices, slot, -1)
    away_k = results[1].reshape(span, -1).astype(jnp.bfloat16).reshape(devices, slot, -1)
    away_v = results[2].reshape(span, -1).astype(jnp.bfloat16).reshape(devices, slot, -1)
    heads_local = results[3].shape[2]
    away_log = jnp.transpose(results[3], (2, 0, 1, 3)).reshape(heads_local, span)
    back_q_rows, back_k_rows, back_v_rows = (
        lax.all_to_all(away_q, "dp", split_axis=0, concat_axis=0, tiled=True),
        lax.all_to_all(away_k, "dp", split_axis=0, concat_axis=0, tiled=True),
        lax.all_to_all(away_v, "dp", split_axis=0, concat_axis=0, tiled=True),
    )
    picked = jnp.clip(target, 0, span - 1)
    home_spot = jnp.clip(rank, 0, home_count - 1)
    moving = leaving[:, None]
    dq_norm = jnp.where(
        moving,
        jnp.take(back_q_rows.reshape(span, -1), picked, axis=0),
        jnp.take(home_q.astype(jnp.bfloat16), home_spot, axis=0),
    )
    dk_norm = jnp.where(
        moving,
        jnp.take(back_k_rows.reshape(span, -1), picked, axis=0),
        jnp.take(home_k.astype(jnp.bfloat16), home_spot, axis=0),
    )
    grad_v = jnp.where(
        moving,
        jnp.take(back_v_rows.reshape(span, -1), picked, axis=0),
        jnp.take(home_v.astype(jnp.bfloat16), home_spot, axis=0),
    )
    balanced = jnp.concatenate([home_log, away_log], axis=1)
    scaled_q = dq_norm.astype(jnp.float32) * q_gain[None, :]
    scaled_k = dk_norm.astype(jnp.float32) * k_gain[None, :]
    back_q, back_k = lax.psum(
        (jnp.sum(scaled_q * q_float, axis=1), jnp.sum(scaled_k * k_float, axis=1)), "head"
    )
    cube_q = recip_q * recip_q * recip_q * back_q / width_q
    cube_k = recip_k * recip_k * recip_k * back_k / width_k
    grad_q = (recip_q[:, None] * scaled_q - q_float * cube_q[:, None]).astype(jnp.bfloat16)
    grad_k = (recip_k[:, None] * scaled_k - k_float * cube_k[:, None]).astype(jnp.bfloat16)
    return (grad_q, grad_k, grad_v, balanced)


def solution(mesh):
    in_specs = (
        P("dp", "head"),
        P("dp", "head"),
        P("dp", "head"),
        P("dp", "head"),
        P("head"),
        P("head"),
        P("dp", None),
        P("dp", None),
        P("dp", None),
    )
    out_specs = (P("dp", "head"), P("dp", "head"), P("dp", "head"), P("head", "dp"))
    return jax.shard_map(local, mesh=mesh, in_specs=in_specs, out_specs=out_specs, check_vma=False)
```

profile of v0, /device:TPU:0, one launch (start us, length us, event | category | flops | bytes accessed | tf_op | source)
XLA Modules:
  0.0 556.1 jit_solution(12357021509620325057)
XLA Ops:
  3.8 11.1 %scatter_custom_fusion.1 = bf16[3072]{0:T(1024)(128)(2,1)S(1)} fusion(s32[1536]{0:T(1024)S(1)} %get-tuple-element.122, bf16[1536]{0:T(1024)(128)(2,1)S(1)} %broadcast.415, bf16[]{:T(256)} %constant.142.clone.1), kind=kCustom, calls=%fused_computation.180 | custom fusion | bytes 6146 | tf_op jit(solution)/shard_map/scatter | solution.py:116
  16.8 7.3 %all-to-all-start.1 = ((bf16[8,2,192]{2,1,0:T(2,128)(2,1)}), bf16[8,2,192]{2,1,0:T(2,128)(2,1)S(1)}, u32[]{:S(2)}, u32[]{:S(2)}) async-start(bf16[8,2,192]{2,1,0:T(2,128)(2,1)} %reshape.752), calls=%async_computation.1 | async-start | bytes 16384 | tf_op jit(solution)/shard_map/all_to_all | solution.py:124
  27.4 10.7 %all-reduce.1 = (f32[1536]{0:T(1024)S(1)}, f32[1536]{0:T(1024)S(1)}) all-reduce(f32[1536]{0:T(1024)S(1)} %fusion.31, f32[1536]{0:T(1024)S(1)} %fusion.67), channel_id=1, replica_groups=mesh['dp'=8,'head'=4] {'head'}, use_global_device_ids=true, to_apply=%region_1.0 | all-reduce | flops 3072 | bytes 24576 | tf_op jit(solution)/shard_map/psum | solution.py:80
  38.1 6.2 %scatter_custom_fusion = bf16[3072,128]{1,0:T(8,128)(2,1)} fusion(s32[1536]{0:T(1024)S(1)} %get-tuple-element.122, bf16[]{:T(256)} %constant.142.clone.1, bf16[1536,128]{1,0:T(8,128)(2,1)S(1)} %copy-done.5, f32[128]{0:T(128)} %param.24, f32[1536]{0:T(1024)S(1)} %add_rsqrt_fusion), kind=kCustom, calls=%fused_computation.121 | custom fusion | flops 786432 | bytes 1188354 | tf_op jit(solution)/shard_map/scatter | solution.py:111
  44.3 5.7 %all-to-all-start = ((bf16[8,384,128]{2,1,0:T(8,128)(2,1)}), bf16[8,384,128]{2,1,0:T(8,128)(2,1)S(1)}, u32[]{:S(2)}, u32[]{:S(2)}) async-start(bf16[8,384,128]{2,1,0:T(8,128)(2,1)} %bitcast.45), calls=%async_computation | async-start | bytes 1572864 | tf_op jit(solution)/shard_map/all_to_all | solution.py:121
  50.0 5.7 %scatter_custom_fusion.3 = bf16[3072,128]{1,0:T(8,128)(2,1)} fusion(s32[1536]{0:T(1024)S(1)} %get-tuple-element.122, bf16[1536,128]{1,0:T(8,128)(2,1)} %param.21, bf16[]{:T(256)} %constant.142.clone.1), kind=kCustom, calls=%fused_computation.119 | custom fusion | bytes 786944 | tf_op jit(solution)/shard_map/scatter | solution.py:111
  55.8 13.8 %all-to-all-done = bf16[8,384,128]{2,1,0:T(8,128)(2,1)S(1)} async-done(((bf16[8,384,128]{2,1,0:T(8,128)(2,1)}), bf16[8,384,128]{2,1,0:T(8,128)(2,1)S(1)}, u32[]{:S(2)}, u32[]{:S(2)}) %all-to-all-start) | async-done | bytes 786464 | tf_op jit(solution)/shard_map/all_to_all | solution.py:121
  73.7 11.0 %scatter_custom_fusion.2 = bf16[3072,640]{1,0:T(8,128)(2,1)} fusion(s32[1536]{0:T(1024)S(1)} %get-tuple-element.122, bf16[]{:T(256)} %constant.142.clone.1, bf16[1536,640]{1,0:T(8,128)(2,1)} %param.19, f32[640]{0:T(1024)S(1)} %copy-done.23, f32[1536]{0:T(1024)S(1)} %add_rsqrt_fusion.1), kind=kCustom, calls=%fused_computation.85 | custom fusion | flops 3932160 | bytes 5910530 | tf_op jit(solution)/shard_map/scatter | solution.py:111
  84.6 9.3 %all-to-all-done.3 = bf16[8,384,128]{2,1,0:T(8,128)(2,1)S(1)} async-done(((bf16[8,384,128]{2,1,0:T(8,128)(2,1)}), bf16[8,384,128]{2,1,0:T(8,128)(2,1)S(1)}, u32[]{:S(2)}, u32[]{:S(2)}) %all-to-all-start.3) | async-done | bytes 786464 | tf_op jit(solution)/shard_map/all_to_all | solution.py:122
  98.5 10.4 %scatter_custom_fusion.4 = bf16[3072,640]{1,0:T(8,128)(2,1)} fusion(s32[1536]{0:T(1024)S(1)} %get-tuple-element.122, bf16[1536,640]{1,0:T(8,128)(2,1)} %param.22, bf16[]{:T(256)} %constant.142.clone.1), kind=kCustom, calls=%fused_computation.83 | custom fusion | bytes 3932672 | tf_op jit(solution)/shard_map/scatter | solution.py:111
  108.9 76.5 %all-to-all-done.2 = bf16[8,384,640]{2,1,0:T(8,128)(2,1)} async-done(((bf16[8,384,640]{2,1,0:T(8,128)(2,1)}), bf16[8,384,640]{2,1,0:T(8,128)(2,1)}, u32[]{:S(2)}, u32[]{:S(2)}) %all-to-all-start.2) | async-done | bytes 3932192 | tf_op jit(solution)/shard_map/all_to_all | solution.py:120
  190.4 6.3 %copy.129 = bf16[8,384,640]{1,2,0:T(8,128)(2,1)} copy(bf16[8,384,640]{2,1,0:T(8,128)(2,1)} %all-to-all-done.2) | data formatting | bytes 7864320 | tf_op jit(solution)/shard_map/all_to_all | solution.py:120
  196.7 80.3 %all-to-all-done.4 = bf16[8,384,640]{2,1,0:T(8,128)(2,1)} async-done(((bf16[8,384,640]{2,1,0:T(8,128)(2,1)}), bf16[8,384,640]{2,1,0:T(8,128)(2,1)}, u32[]{:S(2)}, u32[]{:S(2)}) %all-to-all-start.4) | async-done | bytes 3932192 | tf_op jit(solution)/shard_map/all_to_all | solution.py:123
  277.0 107.5 %while.16 = (s32[]{:T(128)}, bf16[4,2,384,640]{2,3,1,0:T(8,128)(2,1)}, bf16[4,2,384,128]{2,3,1,0:T(8,128)(2,1)}, bf16[4,2,384,128]{2,3,1,0:T(8,128)(2,1)}, f32[4...) while((s32[]{:T(128)}, ...), condition=%wide.region_18.19_spmd, body=%wide.region_14.18_spmd.sunk | while | flops 2305933056 | bytes 113494368 | solution.py:161
  314.0 5.6 fusion.153
  340.9 5.6 fusion.153
  391.8 19.1 %all-to-all-done.6 = bf16[8,384,128]{2,1,0:T(8,128)(2,1)S(1)} async-done(((bf16[8,384,128]{2,1,0:T(8,128)(2,1)}), bf16[8,384,128]{2,1,0:T(8,128)(2,1)S(1)}, u32[]{:S(2)}, u32[]{:S(2)}) %all-to-all-start.6) | async-done | bytes 786464 | tf_op jit(solution)/shard_map/all_to_all | solution.py:179
  414.7 6.1 %copy.131 = bf16[8,384,640]{2,1,0:T(8,128)(2,1)} copy(bf16[8,384,640]{1,2,0:T(8,128)(2,1)} %bitcast.340) | data formatting | bytes 7864320 | tf_op jit(solution)/shard_map/convert_element_type | solution.py:172
  420.8 14.1 %all-to-all-done.7 = bf16[8,384,128]{2,1,0:T(8,128)(2,1)S(1)} async-done(((bf16[8,384,128]{2,1,0:T(8,128)(2,1)}), bf16[8,384,128]{2,1,0:T(8,128)(2,1)S(1)}, u32[]{:S(2)}, u32[]{:S(2)}) %all-to-all-start.7) | async-done | bytes 786464 | tf_op jit(solution)/shard_map/all_to_all | solution.py:180
  440.3 6.2 %scatter_custom_fusion.5 = s32[384]{0:T(512)S(1)} fusion(s32[1536]{0:T(1024)S(1)} %get-tuple-element.120, s32[1536]{0:T(1024)S(1)} %iota.75, s32[]{:T(128)} %constant.130.clone.1), kind=kCustom, calls=%fused_computation.185 | custom fusion | bytes 1540 | tf_op jit(solution)/shard_map/scatter | solution.py:106
  497.1 5.8 %gather_fusion.2 = bf16[1536,640]{1,0:T(8,128)(2,1)} fusion(bf16[384,640]{1,0:T(8,128)(2,1)S(1)} %copy.141, s32[2048]{0:T(1024)S(1)} %pad_clamp_fusion.2), kind=kCustom, calls=%fused_computation.10 | custom fusion | bytes 3938304 | tf_op jit(solution)/shard_map/jit(_take)/gather | solution.py:188
  519.3 8.0 %all-to-all-done.5 = bf16[8,384,640]{2,1,0:T(8,128)(2,1)} async-done(((bf16[8,384,640]{2,1,0:T(8,128)(2,1)}), bf16[8,384,640]{2,1,0:T(8,128)(2,1)}, u32[]{:S(2)}, u32[]{:S(2)}) %all-to-all-start.5) | async-done | bytes 3932192 | tf_op jit(solution)/shard_map/all_to_all | solution.py:178
  527.2 8.5 %gather_fusion = bf16[1536,640]{1,0:T(8,128)(2,1)} fusion(bf16[3072,640]{1,0:T(8,128)(2,1)} %bitcast.54, s32[2048]{0:T(1024)S(1)} %pad_clamp_fusion.3), kind=kCustom, calls=%fused_computation.8 | custom fusion | bytes 3938304 | tf_op jit(solution)/shard_map/jit(_take)/gather | solution.py:187
  541.1 10.1 %all-reduce = (f32[1536]{0:T(1024)S(1)}, f32[1536]{0:T(1024)S(1)}) all-reduce(f32[1536]{0:T(1024)S(1)} %get-tuple-element.153, f32[1536]{0:T(1024)S(1)} %get-tuple-element.151), channel_id=1, replica_groups=mesh['dp'=8,'head'=4] {'head'}, use_global_device_ids=true, to_apply=%region_26.29 | all-reduce | flops 3072 | bytes 24576 | tf_op jit(solution)/shard_map/psum | solution.py:203
  (251 shorter events, 210.8 us)
Async XLA Ops:
  0.6 37.4 %copy-start.5 = (bf16[1536,128]{1,0:T(8,128)(2,1)S(1)}, bf16[1536,128]{1,0:T(8,128)(2,1)}, u32[]{:S(2)}) copy-start(bf16[1536,128]{1,0:T(8,128)(2,1)} %param.20) | copy-start | bytes 1179652
  16.8 27.5 %all-to-all-start.1 = ((bf16[8,2,192]{2,1,0:T(2,128)(2,1)}), bf16[8,2,192]{2,1,0:T(2,128)(2,1)S(1)}, u32[]{:S(2)}, u32[]{:S(2)}) async-start(bf16[8,2,192]{2,1,0:T(2,128)(2,1)} %reshape.752), calls=%async_computation.1 | async-start | bytes 16384 | tf_op jit(solution)/shard_map/all_to_all | solution.py:124
  26.1 47.6 %copy-start.23 = (f32[640]{0:T(1024)S(1)}, f32[640]{0:T(1024)}, u32[]{:S(2)}) copy-start(f32[640]{0:T(1024)} %param.23) | copy-start | bytes 7684
  44.3 25.3 %all-to-all-start = ((bf16[8,384,128]{2,1,0:T(8,128)(2,1)}), bf16[8,384,128]{2,1,0:T(8,128)(2,1)S(1)}, u32[]{:S(2)}, u32[]{:S(2)}) async-start(bf16[8,384,128]{2,1,0:T(8,128)(2,1)} %bitcast.45), calls=%async_computation | async-start | bytes 1572864 | tf_op jit(solution)/shard_map/all_to_all | solution.py:121
  69.6 24.4 %all-to-all-start.3 = ((bf16[8,384,128]{2,1,0:T(8,128)(2,1)}), bf16[8,384,128]{2,1,0:T(8,128)(2,1)S(1)}, u32[]{:S(2)}, u32[]{:S(2)}) async-start(bf16[8,384,128]{2,1,0:T(8,128)(2,1)} %bitcast.49), calls=%async_computation.3 | async-start | bytes 1572864 | tf_op jit(solution)/shard_map/all_to_all | solution.py:122
  94.0 91.4 %all-to-all-start.2 = ((bf16[8,384,640]{2,1,0:T(8,128)(2,1)}), bf16[8,384,640]{2,1,0:T(8,128)(2,1)}, u32[]{:S(2)}, u32[]{:S(2)}) async-start(bf16[8,384,640]{2,1,0:T(8,128)(2,1)} %bitcast.336), calls=%async_computation.2 | async-start | bytes 7864320 | tf_op jit(solution)/shard_map/all_to_all | solution.py:120
  185.4 91.7 %all-to-all-start.4 = ((bf16[8,384,640]{2,1,0:T(8,128)(2,1)}), bf16[8,384,640]{2,1,0:T(8,128)(2,1)}, u32[]{:S(2)}, u32[]{:S(2)}) async-start(bf16[8,384,640]{2,1,0:T(8,128)(2,1)} %bitcast.335), calls=%async_computation.4 | async-start | bytes 7864320 | tf_op jit(solution)/shard_map/all_to_all | solution.py:123
  284.8 7.9 %slice-start = ((s8[5898240]{0:T(1024)(128)(4,1)}), s8[1703936]{0:T(1024)(128)(4,1)S(1)}, s32[]{:S(2)}) async-start(s8[5898240]{0:T(1024)(128)(4,1)} %bitcast.324), calls=%async_computation.8 | async-start | bytes 3407872 | tf_op jit(solution)/shard_map/while
  311.6 7.9 %slice-start = ((s8[5898240]{0:T(1024)(128)(4,1)}), s8[1703936]{0:T(1024)(128)(4,1)S(1)}, s32[]{:S(2)}) async-start(s8[5898240]{0:T(1024)(128)(4,1)} %bitcast.324), calls=%async_computation.8 | async-start | bytes 3407872 | tf_op jit(solution)/shard_map/while
  314.0 5.6 %copy-start.2 = (bf16[1,2,384,640]{2,3,1,0:T(8,128)(2,1)S(1)}, bf16[1,2,384,640]{2,3,1,0:T(8,128)(2,1)}, u32[]{:S(2)}) copy-start(bf16[1,2,384,640]{2,3,1,0:T(8,128)(2,1)} %copy.180) | copy-start | bytes 2949124 | tf_op jit(solution)/shard_map/while
  338.6 7.9 %slice-start = ((s8[5898240]{0:T(1024)(128)(4,1)}), s8[1703936]{0:T(1024)(128)(4,1)S(1)}, s32[]{:S(2)}) async-start(s8[5898240]{0:T(1024)(128)(4,1)} %bitcast.324), calls=%async_computation.8 | async-start | bytes 3407872 | tf_op jit(solution)/shard_map/while
  365.5 7.9 %slice-start = ((s8[5898240]{0:T(1024)(128)(4,1)}), s8[1703936]{0:T(1024)(128)(4,1)S(1)}, s32[]{:S(2)}) async-start(s8[5898240]{0:T(1024)(128)(4,1)} %bitcast.324), calls=%async_computation.8 | async-start | bytes 3407872 | tf_op jit(solution)/shard_map/while
  384.6 6.0 %copy-start.19 = (bf16[4,2,384,128]{2,3,1,0:T(8,128)(2,1)S(1)}, bf16[4,2,384,128]{2,3,1,0:T(8,128)(2,1)}, u32[]{:S(2)}) copy-start(bf16[4,2,384,128]{2,3,1,0:T(8,128)(2,1)} %get-tuple-element.70) | copy-start | bytes 2359300
  386.9 24.0 %all-to-all-start.6 = ((bf16[8,384,128]{2,1,0:T(8,128)(2,1)}), bf16[8,384,128]{2,1,0:T(8,128)(2,1)S(1)}, u32[]{:S(2)}, u32[]{:S(2)}) async-start(bf16[8,384,128]{2,1,0:T(8,128)(2,1)} %copy.142), calls=%async_computation.6 | async-start | bytes 1572864 | tf_op jit(solution)/shard_map/all_to_all | solution.py:179
  410.9 23.9 %all-to-all-start.7 = ((bf16[8,384,128]{2,1,0:T(8,128)(2,1)}), bf16[8,384,128]{2,1,0:T(8,128)(2,1)S(1)}, u32[]{:S(2)}, u32[]{:S(2)}) async-start(bf16[8,384,128]{2,1,0:T(8,128)(2,1)} %copy.145), calls=%async_computation.7 | async-start | bytes 1572864 | tf_op jit(solution)/shard_map/all_to_all | solution.py:180
  435.8 91.4 %all-to-all-start.5 = ((bf16[8,384,640]{2,1,0:T(8,128)(2,1)}), bf16[8,384,640]{2,1,0:T(8,128)(2,1)}, u32[]{:S(2)}, u32[]{:S(2)}) async-start(bf16[8,384,640]{2,1,0:T(8,128)(2,1)} %copy.131), calls=%async_computation.5 | async-start | bytes 7864320 | tf_op jit(solution)/shard_map/all_to_all | solution.py:178
  446.5 7.3 %copy-start.11 = (bf16[1536,128]{1,0:T(8,128)(2,1)S(1)}, bf16[1536,128]{1,0:T(8,128)(2,1)}, u32[]{:S(2)}) copy-start(bf16[1536,128]{1,0:T(8,128)(2,1)} %param.21) | copy-start | bytes 1179652
  449.1 6.6 %copy-start.1 = (bf16[1536,640]{1,0:T(8,128)(2,1)S(1)}, bf16[1536,640]{1,0:T(8,128)(2,1)}, u32[]{:S(2)}) copy-start(bf16[1536,640]{1,0:T(8,128)(2,1)} %param.19) | copy-start | bytes 5898244
  462.0 8.7 %copy-start.6 = (bf16[1536,128]{1,0:T(8,128)(2,1)S(1)}, bf16[1536,128]{1,0:T(8,128)(2,1)}, u32[]{:S(2)}) copy-start(bf16[1536,128]{1,0:T(8,128)(2,1)} %param.20) | copy-start | bytes 1179652
  462.0 8.7 %copy-start.24 = (f32[128]{0:T(128)S(1)}, f32[128]{0:T(128)}, u32[]{:S(2)}) copy-start(f32[128]{0:T(128)} %param.24) | copy-start | bytes 1540
  497.1 5.8 %copy-start.22 = (f32[4,2,5,384]{3,2,1,0:T(8,128)S(1)}, f32[4,2,5,384]{3,2,1,0:T(8,128)}, u32[]{:S(2)}) copy-start(f32[4,2,5,384]{3,2,1,0:T(8,128)} %get-tuple-element.71) | copy-start | bytes 184324
  503.6 9.0 %copy-start.7 = (bf16[1536,128]{1,0:T(8,128)(2,1)S(1)}, bf16[1536,128]{1,0:T(8,128)(2,1)}, u32[]{:S(2)}) copy-start(bf16[1536,128]{1,0:T(8,128)(2,1)} %param.20) | copy-start | bytes 1179652
  507.6 8.3 %copy-start.12 = (bf16[1536,128]{1,0:T(8,128)(2,1)S(1)}, bf16[1536,128]{1,0:T(8,128)(2,1)}, u32[]{:S(2)}) copy-start(bf16[1536,128]{1,0:T(8,128)(2,1)} %gather_fusion.10) | copy-start | bytes 1179652
  535.8 15.5 %copy-start.14 = (bf16[1536,128]{1,0:T(8,128)(2,1)S(1)}, bf16[1536,128]{1,0:T(8,128)(2,1)}, u32[]{:S(2)}) copy-start(bf16[1536,128]{1,0:T(8,128)(2,1)} %get-tuple-element.152) | copy-start | bytes 1179652
  (35 other events, 119.4 us)
where the time goes:
time: 565 us; the launch traced here: 556 us
  waiting for transfers between devices  221 us (39%)
  local copies, waits for them, and re-layouts  141 us (25%)
  matrix products  75.9 us (13%)
  other arithmetic  57.5 us (10%)
  starting transfers between devices  38.2 us (7%)
  blocking collectives  20.8 us (4%)
    all_to_all x1, waiting for transfers between devices, local(): lax.all_to_all(to_slots(d_out), 'dp', split_axis=0, concat_axis=0, tiled=...  80.3 us
    all_to_all x1, waiting for transfers between devices, local(): lax.all_to_all(to_slots(q_norm), 'dp', split_axis=0, concat_axis=0, tiled...  76.5 us
    dot_general x5, matrix products, block_backward(): jnp.einsum('gjqk,qgjd->kgd', weights_low, upstream, preferred_element_typ...  25.7 us
    dynamic_slice x12, local copies, waits for them, and re-layouts, local(): lax.map(tile_group, (grouped(got_q.reshape(span, -1)), grouped(got_k.resh...  24.1 us
    all_to_all x1, waiting for transfers between devices, local(): lax.all_to_all(away_k, 'dp', split_axis=0, concat_axis=0, tiled=True)  19.1 us
    scatter x2, other arithmetic, to_slots(): empty.at[target].set(rows, mode='drop')  17.2 us
    scatter x2, local copies, waits for them, and re-layouts, to_slots(): empty.at[target].set(rows, mode='drop')  16.1 us
    dot_general x5, matrix products, block_backward(): jnp.einsum('qgjd,kgd->gjqk', upstream, value_heads, preferred_element_typ...  14.6 us
  transfers between devices with their start and end apart: 8, of which 7 were waited for; matrix products, arithmetic and copies ran while one was open for 23% of the time, Pallas kernels for 0%

commit v1 on v0

v1 whole, which is shorter than its diff:
```python
import functools
import math

import jax
import jax.numpy as jnp
from jax import lax
from jax.experimental import pallas as pl
from jax.experimental.pallas import tpu as pltpu
from jax.sharding import PartitionSpec as P

HDIM = 128
ROWS = 128
REACH = 384

eps = 1e-06
big_negative = -1e30


def column(row):
    return jnp.transpose(jnp.broadcast_to(row, (ROWS, ROWS)))


def row_sums(tile):
    return jnp.sum(jnp.transpose(tile), axis=0, keepdims=True)


def nt_dot(a, b):
    return lax.dot_general(a, b, (((1,), (1,)), ((), ())), preferred_element_type=jnp.float32)


def attention_kernel(
    docs,
    devices,
    slot,
    home_count,
    len_ref,
    dest_ref,
    off_ref,
    q_ref,
    grad_ref,
    k_ref,
    v_ref,
    recip_q_ref,
    recip_k_ref,
    q_gain_ref,
    k_gain_ref,
    dq_ref,
    dk_ref,
    dv_ref,
    back_ref,
    home_ref,
    slots_ref,
    kn_ref,
    kn_t_ref,
    dk_acc,
    dv_acc,
    lse_ref,
):
    step = pl.program_id(0)
    seq_len = k_ref.shape[0]
    blocks = seq_len // ROWS
    heads = q_ref.shape[1] // HDIM
    scaling = 1.0 / math.sqrt(HDIM)
    here = lax.axis_index("dp")

    @pl.when(step == 0)
    def _():
        dk_acc[...] = jnp.zeros_like(dk_acc)
        dv_acc[...] = jnp.zeros_like(dv_acc)
        lse_ref[...] = jnp.zeros_like(lse_ref)
        for b in range(blocks):
            at = slice(b * ROWS, (b + 1) * ROWS)
            normed = (
                k_ref[at, :].astype(jnp.float32)
                * column(recip_k_ref[b : b + 1, :])
                * k_gain_ref[...]
            )
            low = normed.astype(jnp.bfloat16)
            kn_ref[at, :] = low
            kn_t_ref[:, at] = jnp.transpose(low.astype(jnp.float32)).astype(jnp.bfloat16)

    base = step * ROWS
    token = base + lax.broadcasted_iota(jnp.int32, (1, ROWS), 1)
    start = jnp.zeros((1, ROWS), jnp.int32)
    first = jnp.int32(0)
    end = jnp.int32(0)
    for j in range(docs):
        end = end + len_ref[0, j]
        start = jnp.where(token >= end, end, start)
        first = jnp.where(base >= end, end, first)
    needed = step - first // ROWS + 1

    def block(count):
        width = count * ROWS
        key_at = pl.multiple_of((step - (count - 1)) * ROWS, ROWS)
        window = pl.ds(key_at, width)
        recip = column(recip_q_ref[pl.ds(step, 1), :])
        normed, upstream = [], []
        for h in range(heads):
            lanes = slice(h * HDIM, (h + 1) * HDIM)
            tile = q_ref[:, lanes].astype(jnp.float32) * recip * q_gain_ref[:, lanes]
            normed.append(tile.astype(jnp.bfloat16))
            upstream.append(grad_ref[:, lanes])
        queries = jnp.concatenate(normed, axis=0)
        grads = jnp.concatenate(upstream, axis=0)
        scores = nt_dot(kn_ref[window, :], queries)
        grad_weights = nt_dot(v_ref[window, :], grads)
        key = key_at + lax.broadcasted_iota(jnp.int32, (width, ROWS), 0)
        bias = jnp.where((key >= start) & (key <= token), 0.0, big_negative)
        weights_all, grad_all = [], []
        for h in range(heads):
            lanes = slice(h * HDIM, (h + 1) * HDIM)
            logits = scores[:, lanes] * (scaling * math.log2(math.e)) + bias
            peak = jnp.max(logits, axis=0, keepdims=True)
            powers = jnp.exp2(logits - peak)
            total = jnp.sum(powers, axis=0, keepdims=True)
            lse_ref[h : h + 1, pl.ds(pl.multiple_of(base, ROWS), ROWS)] = (
                peak * math.log(2.0) + jnp.log(total)
            )
            weights = powers * (1.0 / total)
            low = weights.astype(jnp.bfloat16)
            upper = grad_weights[:, lanes]
            delta = jnp.sum(low.astype(jnp.float32) * upper, axis=0, keepdims=True)
            weights_all.append(low)
            grad_all.append((weights * (upper - delta) * scaling).astype(jnp.bfloat16))
        weights_low = jnp.concatenate(weights_all, axis=1)
        grad_low = jnp.concatenate(grad_all, axis=1)
        dv_acc[window, :] += jnp.dot(weights_low, grads, preferred_element_type=jnp.float32)
        dk_acc[window, :] += jnp.dot(grad_low, queries, preferred_element_type=jnp.float32)
        dq_t = jnp.dot(kn_t_ref[:, window], grad_low, preferred_element_type=jnp.float32)
        inner = jnp.zeros((ROWS, HDIM), jnp.float32)
        for h in range(heads):
            lanes = slice(h * HDIM, (h + 1) * HDIM)
            low = jnp.transpose(dq_t[:, lanes]).astype(jnp.bfloat16)
            dq_ref[:, lanes] = low
            inner += low.astype(jnp.float32) * q_gain_ref[:, lanes] * q_ref[:, lanes].astype(
                jnp.float32
            )
        back_ref[pl.ds(step, 1), :] = row_sums(inner)

    for count in range(1, REACH // ROWS + 2):
        pl.when(needed == count)(functools.partial(block, count))

    @pl.when(step == blocks - 1)
    def _():
        dv_ref[...] = dv_acc[...].astype(jnp.bfloat16)
        for b in range(blocks):
            at = slice(b * ROWS, (b + 1) * ROWS)
            low = dk_acc[at, :].astype(jnp.bfloat16)
            dk_ref[at, :] = low
            back_ref[blocks + b : blocks + b + 1, :] = row_sums(
                low.astype(jnp.float32) * k_gain_ref[...] * k_ref[at, :].astype(jnp.float32)
            )
        slots_ref[...] = jnp.zeros_like(slots_ref)
        logs = lse_ref[...]
        home = jnp.zeros((8, home_count), jnp.float32)
        kept = jnp.int32(0)
        begin = jnp.int32(0)
        home_at = lax.broadcasted_iota(jnp.int32, (8, home_count), 1)
        for j in range(docs):
            length = len_ref[0, j]
            dest = dest_ref[0, j]
            stays = dest == here
            shift = jnp.where(stays, kept, off_ref[0, j])
            turned = pltpu.roll(logs, lax.rem(shift - begin + seq_len, seq_len), 1)
            inside = (home_at >= shift) & (home_at < shift + length)
            piece = jnp.where(inside, turned[:, :home_count], 0.0)
            home += jnp.where(stays, piece, 0.0)

            @pl.when(jnp.logical_not(stays))
            def _():
                slots_ref[dest] = piece[:, :slot]

            kept = kept + jnp.where(stays, length, 0)
            begin = begin + length
        home_ref[...] = home


def attention(q, k, v, d_out, recip_q, recip_k, q_gain, k_gain, lengths, dest, offset, devices, slot):
    seq_len, width = q.shape
    blocks = seq_len // ROWS
    home_count = seq_len // 4
    smem = pl.BlockSpec(memory_space=pltpu.SMEM)

    def whole(shape):
        return pl.BlockSpec(shape, lambda i: (0,) * len(shape))

    rows = pl.BlockSpec((ROWS, width), lambda i: (i, 0))
    kv = whole((seq_len, HDIM))
    return pl.pallas_call(
        functools.partial(attention_kernel, lengths.shape[1], devices, slot, home_count),
        grid=(blocks,),
        in_specs=[
            smem,
            smem,
            smem,
            rows,
            rows,
            kv,
            kv,
            whole((blocks, ROWS)),
            whole((blocks, ROWS)),
            whole((1, width)),
            whole((1, HDIM)),
        ],
        out_specs=[
            rows,
            kv,
            kv,
            whole((2 * blocks, ROWS)),
            whole((8, home_count)),
            whole((devices, 8, slot)),
        ],
        out_shape=[
            jax.ShapeDtypeStruct((seq_len, width), jnp.bfloat16),
            jax.ShapeDtypeStruct((seq_len, HDIM), jnp.bfloat16),
            jax.ShapeDtypeStruct((seq_len, HDIM), jnp.bfloat16),
            jax.ShapeDtypeStruct((2 * blocks, ROWS), jnp.float32),
            jax.ShapeDtypeStruct((8, home_count), jnp.float32),
            jax.ShapeDtypeStruct((devices, 8, slot), jnp.float32),
        ],
        scratch_shapes=[
            pltpu.VMEM((seq_len, HDIM), jnp.bfloat16),
            pltpu.VMEM((HDIM, seq_len), jnp.bfloat16),
            pltpu.VMEM((seq_len, HDIM), jnp.float32),
            pltpu.VMEM((seq_len, HDIM), jnp.float32),
            pltpu.VMEM((8, seq_len), jnp.float32),
        ],
        compiler_params=pltpu.CompilerParams(
            vmem_limit_bytes=48 * 1024 * 1024, dimension_semantics=("arbitrary",)
        ),
        cost_estimate=pl.CostEstimate(
            flops=10 * seq_len * REACH * width,
            bytes_accessed=8 * seq_len * width,
            transcendentals=seq_len * REACH * width // HDIM,
        ),
    )(lengths, dest, offset, q, d_out, k, v, recip_q, recip_k, q_gain, k_gain)


def local(q_raw, k_raw, v_proj, d_out, q_gain, k_gain, doc_lengths, plan_dest, plan_offset):
    seq_len = q_raw.shape[0]
    heads = q_raw.shape[1] // HDIM
    blocks = seq_len // ROWS
    devices = lax.axis_size("dp")
    span = 2 * seq_len
    slot = span // devices
    width_q = q_raw.shape[1] * lax.axis_size("head")
    width_k = k_raw.shape[1] * lax.axis_size("head")
    q_float = q_raw.astype(jnp.float32)
    k_float = k_raw.astype(jnp.float32)
    sums = lax.psum(
        jnp.stack([jnp.sum(q_float * q_float, axis=1), jnp.sum(k_float * k_float, axis=1)]), "head"
    )
    recip_q = lax.rsqrt(sums[0] / width_q + eps)
    recip_k = lax.rsqrt(sums[1] / width_k + eps)
    dq_norm, dk_norm, grad_v, back, home_log, slots = attention(
        q_raw,
        k_raw,
        v_proj,
        d_out,
        recip_q.reshape(blocks, ROWS),
        recip_k.reshape(blocks, ROWS),
        q_gain.reshape(1, -1),
        k_gain.reshape(1, -1),
        doc_lengths,
        plan_dest,
        plan_offset,
        devices,
        slot,
    )
    got = lax.all_to_all(slots, "dp", split_axis=0, concat_axis=0, tiled=True)
    away_log = jnp.transpose(got[:, :heads, :], (1, 0, 2)).reshape(heads, span)
    balanced = jnp.concatenate([home_log[:heads], away_log], axis=1)
    back = lax.psum(back, "head").reshape(2, seq_len)
    cube_q = recip_q * recip_q * recip_q * back[0] / width_q
    cube_k = recip_k * recip_k * recip_k * back[1] / width_k
    scaled_q = dq_norm.astype(jnp.float32) * q_gain[None, :]
    scaled_k = dk_norm.astype(jnp.float32) * k_gain[None, :]
    grad_q = (recip_q[:, None] * scaled_q - q_float * cube_q[:, None]).astype(jnp.bfloat16)
    grad_k = (recip_k[:, None] * scaled_k - k_float * cube_k[:, None]).astype(jnp.bfloat16)
    return (grad_q, grad_k, grad_v, balanced)


def solution(mesh):
    in_specs = (
        P("dp", "head"),
        P("dp", "head"),
        P("dp", "head"),
        P("dp", "head"),
        P("head"),
        P("head"),
        P("dp", None),
        P("dp", None),
        P("dp", None),
    )
    out_specs = (P("dp", "head"), P("dp", "head"), P("dp", "head"), P("head", "dp"))
    return jax.shard_map(local, mesh=mesh, in_specs=in_specs, out_specs=out_specs, check_vma=False)
```

time: 565 us -> 59.4 us (0.11); the launches traced: 556 us -> 59.4 us
  waiting for transfers between devices: 221 us -> 0.01 us
  local copies, waits for them, and re-layouts: 141 us -> 2.31 us
  matrix products: 75.9 us -> 0 us
  other arithmetic: 57.5 us -> 8.58 us
  starting transfers between devices: 38.2 us -> 6.04 us
  Pallas kernels: 0 us -> 18.7 us
    all_to_all x8 -> x1, waiting for transfers between devices: 221 us -> 0.01 us  [local(): got = lax.all_to_all(slots, 'dp', split_axis=0, concat_axis=0, tiled=True)]
    dot_general x30 -> x0, matrix products: 75.9 us -> none  [the longest x5 25.7 us: block_backward(): jnp.einsum('gjqk,qgjd->kgd', weights_low, upstream, preferred_element_typ...]
    gather x11 -> x0, local copies, waits for them, and re-layouts: 47.3 us -> none  [the longest x1 8.53 us: local(): jnp.take(back_q_rows.reshape(span, -1), picked, axis=0)]
    scatter x4 -> x0, local copies, waits for them, and re-layouts: 33.4 us -> none  [the longest x2 16.1 us: to_slots(): empty.at[target].set(rows, mode='drop')]
    all_to_all x8 -> x1, starting transfers between devices: 38.2 us -> 6.04 us  [local(): got = lax.all_to_all(slots, 'dp', split_axis=0, concat_axis=0, tiled=True)]
    dynamic_slice x12 -> x0, local copies, waits for them, and re-layouts: 24.1 us -> none  [local(): lax.map(tile_group, (grouped(got_q.reshape(span, -1)), grouped(got_k.resh...]
    pallas_call x0 -> x1, Pallas kernels: none -> 18.7 us  [attention(): pl.pallas_call(functools.partial(attention_kernel, lengths.shape[1], devi...]
    scatter x2 -> x0, other arithmetic: 17.2 us -> none  [to_slots(): empty.at[target].set(rows, mode='drop')]
  transfers between devices with their start and end apart: 8 -> 1, of which waited for: 7 -> 0; matrix products, arithmetic and copies ran while one was open for 23% -> 7% of each run, Pallas kernels for 0% -> 0%
where the time goes in v1:
time: 59.4 us
  blocking collectives  23.1 us (39%)
  Pallas kernels  18.7 us (31%)
  other arithmetic  8.58 us (14%)
  starting transfers between devices  6.04 us (10%)
  local copies, waits for them, and re-layouts  2.31 us (4%)
  between operations  0.8 us (1%)
    pallas_call x1, Pallas kernels, attention(): pl.pallas_call(functools.partial(attention_kernel, lengths.shape[1], devi...  18.7 us
    psum x1, blocking collectives, local(): lax.psum(jnp.stack([jnp.sum(q_float * q_float, axis=1), jnp.sum(k_float *...  12.6 us
    psum x1, blocking collectives, local(): back = lax.psum(back, 'head').reshape(2, seq_len)  10.4 us
    all_to_all x1, starting transfers between devices, local(): got = lax.all_to_all(slots, 'dp', split_axis=0, concat_axis=0, tiled=True)  6.04 us
    convert_element_type x1, other arithmetic, local(): (recip_q[:, None] * scaled_q - q_float * cube_q[:, None]).astype(jnp.bflo...  3.21 us
    unnamed x18, local copies, waits for them, and re-layouts  2.29 us
    reduce_sum x1, other arithmetic, local(): jnp.sum(q_float * q_float, axis=1)  2 us
    reduce_sum x1, other arithmetic, local(): jnp.sum(k_float * k_float, axis=1)  1.42 us
  transfers between devices with their start and end apart: 1, of which 0 were waited for; matrix products, arithmetic and copies ran while one was open for 7% of the time, Pallas kernels for 0%

profile of v1, /device:TPU:0, one launch (start us, length us, event | category | flops | bytes accessed | tf_op | source)
XLA Modules:
  0.0 59.4 jit_solution(6143618810993915382)
XLA Ops:
  0.6 0.0 copy-start.2
  0.6 0.0 copy-start
  0.7 0.0 copy-start.8
  0.7 0.0 copy-start.3
  0.7 0.0 copy-start.5
  0.7 0.0 copy-start.6
  0.7 0.0 copy-start.7
  0.7 1.4 %fusion.3 = f32[1536]{0:T(1024)S(1)} fusion(bf16[1536,128]{1,0:T(8,128)(2,1)} %k_ref.1), kind=kLoop, calls=%fused_computation.7 | loop fusion | flops 588288 | bytes 399360 | tf_op jit(solution)/shard_map/reduce_sum | solution.py:252
  2.1 2.0 %fusion = f32[1536]{0:T(1024)S(1)} fusion(bf16[1536,640]{1,0:T(8,128)(2,1)} %q_ref.1), kind=kLoop, calls=%fused_computation.2 | loop fusion | flops 2947584 | bytes 1972224 | tf_op jit(solution)/shard_map/reduce_sum | solution.py:252
  4.2 12.6 %psum.14 = f32[2,1536]{1,0:T(2,128)S(1)} all-reduce(f32[2,1536]{1,0:T(2,128)S(1)} %pad_maximum_fusion.1), channel_id=1, replica_groups=mesh['dp'=8,'head'=4] {'head'}, use_global_device_ids=true, to_apply=%region_2.0 | all-reduce | flops 3072 | bytes 24576 | tf_op jit(solution)/shard_map/psum | solution.py:251
  16.9 0.0 copy-done.8
  16.9 0.0 copy-done.2
  16.9 0.0 copy-done
  16.9 0.0 copy-done.3
  17.0 0.0 copy-start.4
  17.0 1.0 %copy-done.4 = bf16[1536,128]{1,0:T(8,128)(2,1)S(1)} copy-done((bf16[1536,128]{1,0:T(8,128)(2,1)S(1)}, bf16[1536,128]{1,0:T(8,128)(2,1)}, u32[]{:S(2)}) %copy-start.4) | copy-done | bytes 393240
  18.0 18.7 %shard_map.120 = (bf16[1536,640]{1,0:T(8,128)(2,1)S(1)}, bf16[1536,128]{1,0:T(8,128)(2,1)S(1)}, bf16[1536,128]{1,0:T(8,128)(2,1)}, f32[24,128]{1,0:T(8,128)S(1)}...) custom-call(s32[1,8]{1,0:T(1,128)S(1)} %copy-done.5, s32[1,8]{1,0:T(1,128)S(1)} %copy-done.6, s32[1,8]{1,0:T(1,128)S(1)} %copy-done.7, ...), custom_call_target="tpu_custom_call" | custom-call | flops 3774873600 | bytes 7864320 | tf_op jit(solution)/shard_map/pallas_call | solution.py:190
  36.6 1.3 %copy-done.1 = bf16[1536,640]{1,0:T(8,128)(2,1)} copy-done((bf16[1536,640]{1,0:T(8,128)(2,1)}, bf16[1536,640]{1,0:T(8,128)(2,1)S(1)}, u32[]{:S(2)}) %copy-start.1) | copy-done | bytes 1966104
  37.9 6.0 %all-to-all-start = ((f32[8,8,384]{2,1,0:T(8,128)}), f32[8,8,384]{2,1,0:T(8,128)S(1)}, u32[]{:S(2)}, u32[]{:S(2)}) async-start(f32[8,8,384]{2,1,0:T(8,128)} %get-tuple-element.15), calls=%async_computation | async-start | bytes 196608 | tf_op jit(solution)/shard_map/all_to_all | solution.py:271
  43.9 10.4 %psum.15 = f32[24,128]{1,0:T(8,128)S(1)} all-reduce(f32[24,128]{1,0:T(8,128)S(1)} %get-tuple-element.11), channel_id=1, replica_groups=mesh['dp'=8,'head'=4] {'head'}, use_global_device_ids=true, to_apply=%region_3.0 | all-reduce | flops 3072 | bytes 24576 | tf_op jit(solution)/shard_map/psum | solution.py:274
  54.3 3.2 %fusion.2 = bf16[1536,640]{1,0:T(8,128)(2,1)} fusion(bf16[1536,640]{1,0:T(8,128)(2,1)S(1)} %copy-done, bf16[1536,640]{1,0:T(8,128)(2,1)} %copy-done.1, f32[1536]{0:T(1024)S(1)} %get-tuple-element.19, f32[640]{0:T(1024)S(1)} %copy-done.8, f32[1536]{0:T(1024)S(1)} %get-tuple-element.17), kind=kLoop, calls=%fused_computation.4 | loop fusion | flops 6881280 | bytes 5913088 | tf_op jit(solution)/shard_map/convert_element_type | solution.py:279
  57.6 1.2 %fusion.5 = bf16[1536,128]{1,0:T(8,128)(2,1)} fusion(bf16[1536,128]{1,0:T(8,128)(2,1)S(1)} %copy-done.2, bf16[1536,128]{1,0:T(8,128)(2,1)S(1)} %get-tuple-element.12, f32[1536]{0:T(1024)S(1)} %get-tuple-element.18, f32[128]{0:T(128)S(1)} %copy-done.3, f32[1536]{0:T(1024)S(1)} %get-tuple-element.16), kind=kLoop, calls=%fused_computation.9 | loop fusion | flops 1376256 | bytes 1192448 | tf_op jit(solution)/shard_map/convert_element_type | solution.py:280
  58.8 0.0 all-to-all-done
  58.8 0.7 %pad_maximum_fusion = f32[5,3456]{1,0:T(8,128)} fusion(f32[5,3072]{1,0:T(8,128)S(1)} %bitcast.20, f32[5,384]{1,0:T(8,128)S(1)} %bitcast.18), kind=kLoop, calls=%fused_computation.10 | loop fusion | flops 17280 | bytes 138240 | tf_op jit(solution)/shard_map/concatenate | solution.py:273
  (10 shorter events, 0.1 us)
Async XLA Ops:
  0.6 16.3 %copy-start.2 = (bf16[1536,128]{1,0:T(8,128)(2,1)S(1)}, bf16[1536,128]{1,0:T(8,128)(2,1)}, u32[]{:S(2)}) copy-start(bf16[1536,128]{1,0:T(8,128)(2,1)} %k_ref.1) | copy-start | bytes 1179652
  0.6 16.3 %copy-start = (bf16[1536,640]{1,0:T(8,128)(2,1)S(1)}, bf16[1536,640]{1,0:T(8,128)(2,1)}, u32[]{:S(2)}) copy-start(bf16[1536,640]{1,0:T(8,128)(2,1)} %q_ref.1) | copy-start | bytes 5898244
  0.7 16.2 %copy-start.8 = (f32[640]{0:T(1024)S(1)}, f32[640]{0:T(1024)}, u32[]{:S(2)}) copy-start(f32[640]{0:T(1024)} %param.13) | copy-start | bytes 7684
  0.7 16.3 %copy-start.3 = (f32[128]{0:T(128)S(1)}, f32[128]{0:T(128)}, u32[]{:S(2)}) copy-start(f32[128]{0:T(128)} %param.14) | copy-start | bytes 1540
  0.7 16.3 %copy-start.5 = (s32[1,8]{1,0:T(1,128)S(1)}, s32[1,8]{1,0:T(1,128)}, u32[]{:S(2)}) copy-start(s32[1,8]{1,0:T(1,128)} %len_ref.1) | copy-start | bytes 100
  0.7 16.3 %copy-start.6 = (s32[1,8]{1,0:T(1,128)S(1)}, s32[1,8]{1,0:T(1,128)}, u32[]{:S(2)}) copy-start(s32[1,8]{1,0:T(1,128)} %dest_ref.1) | copy-start | bytes 100
  0.7 16.3 %copy-start.7 = (s32[1,8]{1,0:T(1,128)S(1)}, s32[1,8]{1,0:T(1,128)}, u32[]{:S(2)}) copy-start(s32[1,8]{1,0:T(1,128)} %off_ref.1) | copy-start | bytes 100
  17.0 1.0 %copy-start.4 = (bf16[1536,128]{1,0:T(8,128)(2,1)S(1)}, bf16[1536,128]{1,0:T(8,128)(2,1)}, u32[]{:S(2)}) copy-start(bf16[1536,128]{1,0:T(8,128)(2,1)} %v_ref.1) | copy-start | bytes 1179652
  36.6 1.3 %copy-start.1 = (bf16[1536,640]{1,0:T(8,128)(2,1)}, bf16[1536,640]{1,0:T(8,128)(2,1)S(1)}, u32[]{:S(2)}) copy-start(bf16[1536,640]{1,0:T(8,128)(2,1)S(1)} %get-tuple-element.10) | copy-start | bytes 5898244
  37.9 20.9 %all-to-all-start = ((f32[8,8,384]{2,1,0:T(8,128)}), f32[8,8,384]{2,1,0:T(8,128)S(1)}, u32[]{:S(2)}, u32[]{:S(2)}) async-start(f32[8,8,384]{2,1,0:T(8,128)} %get-tuple-element.15), calls=%async_computation | async-start | bytes 196608 | tf_op jit(solution)/shard_map/all_to_all | solution.py:271

commit v2 on v1

--- a/solution.py
+++ b/solution.py
@@ -237,29 +237,180 @@
     )(lengths, dest, offset, q, d_out, k, v, recip_q, recip_k, q_gain, k_gain)
 
 
+def peer_sum(parts_ref, got_ref, send_sem, recv_sem, me, peers):
+    copies = []
+    for d in range(1, peers):
+        copy = pltpu.make_async_remote_copy(
+            src_ref=parts_ref,
+            dst_ref=got_ref.at[d - 1],
+            send_sem=send_sem.at[d - 1],
+            recv_sem=recv_sem.at[d - 1],
+            device_id={"head": lax.rem(me + d, peers)},
+            device_id_type=pl.DeviceIdType.MESH,
+        )
+        copy.start()
+        copies.append(copy)
+    return copies
+
+
+def stat_kernel(peers, q_ref, k_ref, recip_ref, parts_ref, got_ref, send_sem, recv_sem):
+    me = lax.axis_index("head")
+    seq_len, width = q_ref.shape
+    blocks = seq_len // ROWS
+    barrier = pltpu.get_barrier_semaphore()
+    for d in range(1, peers):
+        pl.semaphore_signal(
+            barrier,
+            inc=1,
+            device_id={"head": lax.rem(me + d, peers)},
+            device_id_type=pl.DeviceIdType.MESH,
+        )
+    for b in range(blocks):
+        at = slice(b * ROWS, (b + 1) * ROWS)
+        total = jnp.zeros((ROWS, HDIM), jnp.float32)
+        for h in range(width // HDIM):
+            tile = q_ref[at, h * HDIM : (h + 1) * HDIM].astype(jnp.float32)
+            total += tile * tile
+        parts_ref[b : b + 1, :] = row_sums(total)
+        tile = k_ref[at, :].astype(jnp.float32)
+        parts_ref[blocks + b : blocks + b + 1, :] = row_sums(tile * tile)
+    pl.semaphore_wait(barrier, peers - 1)
+    copies = peer_sum(parts_ref, got_ref, send_sem, recv_sem, me, peers)
+    for copy in copies:
+        copy.wait()
+    sums = parts_ref[...]
+    for d in range(peers - 1):
+        sums += got_ref[d]
+    recip_ref[:blocks, :] = lax.rsqrt(sums[:blocks] / (width * peers) + eps)
+    recip_ref[blocks:, :] = lax.rsqrt(sums[blocks:] / (HDIM * peers) + eps)
+
+
+def token_scales(q, k, peers):
+    blocks = q.shape[0] // ROWS
+    vmem = pl.BlockSpec(memory_space=pltpu.VMEM)
+    return pl.pallas_call(
+        functools.partial(stat_kernel, peers),
+        out_shape=jax.ShapeDtypeStruct((2 * blocks, ROWS), jnp.float32),
+        in_specs=[vmem, vmem],
+        out_specs=vmem,
+        scratch_shapes=[
+            pltpu.VMEM((2 * blocks, ROWS), jnp.float32),
+            pltpu.VMEM((peers - 1, 2 * blocks, ROWS), jnp.float32),
+            pltpu.SemaphoreType.DMA((peers - 1,)),
+            pltpu.SemaphoreType.DMA((peers - 1,)),
+        ],
+        compiler_params=pltpu.CompilerParams(
+            collective_id=0, has_side_effects=True, vmem_limit_bytes=32 * 1024 * 1024
+        ),
+    )(q, k)
+
+
+def finish_kernel(
+    peers,
+    devices,
+    width_q,
+    recip_ref,
+    back_ref,
+    slots_ref,
+    cube_ref,
+    logs_ref,
+    got_ref,
+    log_got_ref,
+    send_sem,
+    recv_sem,
+    log_send_sem,
+    log_recv_sem,
+):
+    me = lax.axis_index("head")
+    here = lax.axis_index("dp")
+    rows = back_ref.shape[0]
+    blocks = rows // 2
+    barrier = pltpu.get_barrier_semaphore()
+    for d in range(1, peers):
+        pl.semaphore_signal(
+            barrier,
+            inc=1,
+            device_id={"head": lax.rem(me + d, peers)},
+            device_id_type=pl.DeviceIdType.MESH,
+        )
+    for d in range(1, devices):
+        pl.semaphore_signal(
+            barrier,
+            inc=1,
+            device_id={"dp": lax.rem(here + d, devices)},
+            device_id_type=pl.DeviceIdType.MESH,
+        )
+    pl.semaphore_wait(barrier, peers - 1 + devices - 1)
+    copies = peer_sum(back_ref, got_ref, send_sem, recv_sem, me, peers)
+    log_copies = []
+    for d in range(1, devices):
+        there = lax.rem(here + d, devices)
+        copy = pltpu.make_async_remote_copy(
+            src_ref=slots_ref.at[there],
+            dst_ref=log_got_ref.at[here],
+            send_sem=log_send_sem.at[d - 1],
+            recv_sem=log_recv_sem.at[d - 1],
+            device_id={"dp": there},
+            device_id_type=pl.DeviceIdType.MESH,
+        )
+        copy.start()
+        log_copies.append(copy)
+    for copy in copies:
+        copy.wait()
+    sums = back_ref[...]
+    for d in range(peers - 1):
+        sums += got_ref[d]
+    recip = recip_ref[...]
+    cubes = recip * recip * recip * sums
+    cube_ref[:blocks, :] = cubes[:blocks] / width_q
+    cube_ref[blocks:, :] = cubes[blocks:] / (HDIM * peers)
+    for copy in log_copies:
+        copy.wait()
+    log_got_ref[here] = jnp.zeros(log_got_ref.shape[1:], jnp.float32)
+    logs_ref[...] = log_got_ref[...]
+
+
+def finish(recip, back, slots, peers, width):
+    devices, pad, slot = slots.shape
+    vmem = pl.BlockSpec(memory_space=pltpu.VMEM)
+    return pl.pallas_call(
+        functools.partial(finish_kernel, peers, devices, width * peers),
+        out_shape=[
+            jax.ShapeDtypeStruct(back.shape, jnp.float32),
+            jax.ShapeDtypeStruct(slots.shape, jnp.float32),
+        ],
+        in_specs=[vmem, vmem, vmem],
+        out_specs=[vmem, vmem],
+        scratch_shapes=[
+            pltpu.VMEM((peers - 1,) + back.shape, jnp.float32),
+            pltpu.VMEM(slots.shape, jnp.float32),
+            pltpu.SemaphoreType.DMA((peers - 1,)),
+            pltpu.SemaphoreType.DMA((peers - 1,)),
+            pltpu.SemaphoreType.DMA((devices - 1,)),
+            pltpu.SemaphoreType.DMA((devices - 1,)),
+        ],
+        compiler_params=pltpu.CompilerParams(
+            collective_id=1, has_side_effects=True, vmem_limit_bytes=32 * 1024 * 1024
+        ),
+    )(recip, back, slots)
+
+
 def local(q_raw, k_raw, v_proj, d_out, q_gain, k_gain, doc_lengths, plan_dest, plan_offset):
     seq_len = q_raw.shape[0]
     heads = q_raw.shape[1] // HDIM
     blocks = seq_len // ROWS
     devices = lax.axis_size("dp")
+    peers = lax.axis_size("head")
     span = 2 * seq_len
     slot = span // devices
-    width_q = q_raw.shape[1] * lax.axis_size("head")
-    width_k = k_raw.shape[1] * lax.axis_size("head")
-    q_float = q_raw.astype(jnp.float32)
-    k_float = k_raw.astype(jnp.float32)
-    sums = lax.psum(
-        jnp.stack([jnp.sum(q_float * q_float, axis=1), jnp.sum(k_float * k_float, axis=1)]), "head"
-    )
-    recip_q = lax.rsqrt(sums[0] / width_q + eps)
-    recip_k = lax.rsqrt(sums[1] / width_k + eps)
+    recip = token_scales(q_raw, k_raw, peers)
     dq_norm, dk_norm, grad_v, back, home_log, slots = attention(
         q_raw,
         k_raw,
         v_proj,
         d_out,
-        recip_q.reshape(blocks, ROWS),
-        recip_k.reshape(blocks, ROWS),
+        recip[:blocks],
+        recip[blocks:],
         q_gain.reshape(1, -1),
         k_gain.reshape(1, -1),
         doc_lengths,
@@ -268,16 +419,17 @@
         devices,
         slot,
     )
-    got = lax.all_to_all(slots, "dp", split_axis=0, concat_axis=0, tiled=True)
+    cubes, got = finish(recip, back, slots, peers, q_raw.shape[1])
     away_log = jnp.transpose(got[:, :heads, :], (1, 0, 2)).reshape(heads, span)
     balanced = jnp.concatenate([home_log[:heads], away_log], axis=1)
-    back = lax.psum(back, "head").reshape(2, seq_len)
-    cube_q = recip_q * recip_q * recip_q * back[0] / width_q
-    cube_k = recip_k * recip_k * recip_k * back[1] / width_k
+    recip = recip.reshape(2, seq_len)
+    cubes = cubes.reshape(2, seq_len)
     scaled_q = dq_norm.astype(jnp.float32) * q_gain[None, :]
     scaled_k = dk_norm.astype(jnp.float32) * k_gain[None, :]
-    grad_q = (recip_q[:, None] * scaled_q - q_float * cube_q[:, None]).astype(jnp.bfloat16)
-    grad_k = (recip_k[:, None] * scaled_k - k_float * cube_k[:, None]).astype(jnp.bfloat16)
+    q_float = q_raw.astype(jnp.float32)
+    k_float = k_raw.astype(jnp.float32)
+    grad_q = (recip[0][:, None] * scaled_q - q_float * cubes[0][:, None]).astype(jnp.bfloat16)
+    grad_k = (recip[1][:, None] * scaled_k - k_float * cubes[1][:, None]).astype(jnp.bfloat16)
     return (grad_q, grad_k, grad_v, balanced)
 
 

time: 59.4 us -> 39.9 us (0.67)
  blocking collectives: 23.1 us -> 0 us
  Pallas kernels: 18.7 us -> 31.9 us
  starting transfers between devices: 6.04 us -> 0 us
  other arithmetic: 8.58 us -> 3.96 us
  local copies, waits for them, and re-layouts: 2.31 us -> 3.57 us
    psum x2 -> x0, blocking collectives: 23.1 us -> none  [the longest x1 12.6 us: local(): lax.psum(jnp.stack([jnp.sum(q_float * q_float, axis=1), jnp.sum(k_float *...]
    pallas_call x0 -> x2, Pallas kernels: none -> 13.9 us  [the longest x1 8.56 us: finish(): pl.pallas_call(functools.partial(finish_kernel, peers, devices, width * p...]
    all_to_all x1 -> x0, starting transfers between devices: 6.04 us -> none  [local(): got = lax.all_to_all(slots, 'dp', split_axis=0, concat_axis=0, tiled=True)]
    reduce_sum x2 -> x0, other arithmetic: 3.42 us -> none  [the longest x1 2 us: local(): jnp.sum(q_float * q_float, axis=1)]
    unnamed x18 -> x20, local copies, waits for them, and re-layouts: 2.29 us -> 3.55 us
    convert_element_type x2, other arithmetic: 4.43 us -> 3.31 us  [the longest x1 2.08 us: local(): (recip[0][:, None] * scaled_q - q_float * cubes[0][:, None]).astype(jnp.b...]
  transfers between devices with their start and end apart: 1 -> 0, of which waited for: 0 -> 0; matrix products, arithmetic and copies ran while one was open for 7% -> 0% of each run, Pallas kernels for 0% -> 0%
where the time goes in v2:
time: 39.9 us; the launch traced here: 40.2 us
  Pallas kernels  31.9 us (80%)
  other arithmetic  3.96 us (10%)
  local copies, waits for them, and re-layouts  3.57 us (9%)
  between operations  0.77 us (2%)
    pallas_call x1, Pallas kernels, attention(): pl.pallas_call(functools.partial(attention_kernel, lengths.shape[1], devi...  18.1 us
    pallas_call x1, Pallas kernels, finish(): pl.pallas_call(functools.partial(finish_kernel, peers, devices, width * p...  8.56 us
    pallas_call x1, Pallas kernels, token_scales(): pl.pallas_call(functools.partial(stat_kernel, peers), out_shape=jax.Shape...  5.3 us
    unnamed x20, local copies, waits for them, and re-layouts  3.55 us
    convert_element_type x1, other arithmetic, local(): (recip[0][:, None] * scaled_q - q_float * cubes[0][:, None]).astype(jnp.b...  2.08 us
    convert_element_type x1, other arithmetic, local(): (recip[1][:, None] * scaled_k - k_float * cubes[1][:, None]).astype(jnp.b...  1.22 us

profile of v2, /device:TPU:0, one launch (start us, length us, event | category | flops | bytes accessed | tf_op | source)
XLA Modules:
  0.0 40.2 jit_solution(11492782600795804675)
XLA Ops:
  0.6 0.0 copy-start
  0.6 1.5 %copy-done = bf16[1536,640]{1,0:T(8,128)(2,1)S(1)} copy-done((bf16[1536,640]{1,0:T(8,128)(2,1)S(1)}, bf16[1536,640]{1,0:T(8,128)(2,1)}, u32[]{:S(2)}) %copy-start) | copy-done | bytes 1966104
  2.2 0.0 copy-start.2
  2.2 1.0 %copy-done.2 = bf16[1536,128]{1,0:T(8,128)(2,1)S(1)} copy-done((bf16[1536,128]{1,0:T(8,128)(2,1)S(1)}, bf16[1536,128]{1,0:T(8,128)(2,1)}, u32[]{:S(2)}) %copy-start.2) | copy-done | bytes 393240
  3.2 0.0 copy-start.9
  3.2 0.0 copy-start.1
  3.2 0.0 copy-start.6
  3.2 0.0 copy-start.7
  3.2 0.0 copy-start.8
  3.2 5.3 %shard_map.120.recip_ref = f32[24,128]{1,0:T(8,128)S(1)} custom-call(bf16[1536,640]{1,0:T(8,128)(2,1)S(1)} %copy-done, bf16[1536,128]{1,0:T(8,128)(2,1)S(1)} %copy-done.2), custom_call_target="tpu_custom_call" | custom-call | tf_op jit(solution)/shard_map/pallas_call | solution.py:291
  8.5 0.0 copy-done.9
  8.6 0.0 copy-done.1
  8.6 0.0 copy-done.3
  8.6 0.0 copy-done.4
  8.6 0.0 copy-done.6
  8.6 0.0 copy-done.7
  8.6 0.0 copy-done.8
  8.6 0.0 copy-start.5
  8.6 1.0 %copy-done.5 = bf16[1536,128]{1,0:T(8,128)(2,1)S(1)} copy-done((bf16[1536,128]{1,0:T(8,128)(2,1)S(1)}, bf16[1536,128]{1,0:T(8,128)(2,1)}, u32[]{:S(2)}) %copy-start.5) | copy-done | bytes 393240
  9.6 18.1 %shard_map.121 = (bf16[1536,640]{1,0:T(8,128)(2,1)S(1)}, bf16[1536,128]{1,0:T(8,128)(2,1)S(1)}, bf16[1536,128]{1,0:T(8,128)(2,1)}, f32[24,128]{1,0:T(8,128)S(1)}...) custom-call(s32[1,8]{1,0:T(1,128)S(1)} %copy-done.6, s32[1,8]{1,0:T(1,128)S(1)} %copy-done.7, s32[1,8]{1,0:T(1,128)S(1)} %copy-done.8, ...), custom_call_target="tpu_custom_call" | custom-call | flops 3774873600 | bytes 7864320 | tf_op jit(solution)/shard_map/pallas_call | solution.py:190
  27.7 8.6 %shard_map.122 = (f32[24,128]{1,0:T(8,128)S(1)}, f32[8,8,384]{2,1,0:T(8,128)S(1)}) custom-call(f32[24,128]{1,0:T(8,128)S(1)} %shard_map.120.recip_ref, f32[24,128]{1,0:T(8,128)S(1)} %get-tuple-element.13.back_ref, f32[8,8,384]{2,1,0:T(8,128)S(1)} %get-tuple-element.14.slots_ref), custom_call_target="tpu_custom_call" | custom-call | tf_op jit(solution)/shard_map/pallas_call | solution.py:376
  36.3 0.7 %pad_maximum_fusion = f32[5,3456]{1,0:T(8,128)} fusion(f32[5,3072]{1,0:T(8,128)S(1)} %bitcast.14, f32[5,384]{1,0:T(8,128)S(1)} %bitcast.15), kind=kLoop, calls=%fused_computation.2 | loop fusion | flops 17280 | bytes 138240 | tf_op jit(solution)/shard_map/concatenate | solution.py:424
  36.9 1.2 %subtract_convert_fusion.1 = bf16[1536,128]{1,0:T(8,128)(2,1)} fusion(bf16[1536,128]{1,0:T(8,128)(2,1)S(1)} %copy-done.3, bf16[1536,128]{1,0:T(8,128)(2,1)S(1)} %get-tuple-element.16, f32[1536]{0:T(1024)S(1)} %get-tuple-element.24, f32[128]{0:T(128)S(1)} %copy-done.4, f32[1536]{0:T(1024)S(1)} %get-tuple-element.20), kind=kLoop, calls=%fused_computation.1 | loop fusion | flops 1376256 | bytes 1192448 | tf_op jit(solution)/shard_map/convert_element_type | solution.py:432
  38.2 2.1 %subtract_convert_fusion = bf16[1536,640]{1,0:T(8,128)(2,1)} fusion(bf16[1536,640]{1,0:T(8,128)(2,1)S(1)} %copy-done.1, bf16[1536,640]{1,0:T(8,128)(2,1)S(1)} %get-tuple-element.12, f32[1536]{0:T(1024)S(1)} %get-tuple-element.25, f32[640]{0:T(1024)S(1)} %copy-done.9, f32[1536]{0:T(1024)S(1)} %get-tuple-element.21), kind=kLoop, calls=%fused_computation | loop fusion | flops 6881280 | bytes 5913088 | tf_op jit(solution)/shard_map/convert_element_type | solution.py:431
  (5 shorter events, 0.0 us)
Async XLA Ops:
  0.6 1.5 %copy-start = (bf16[1536,640]{1,0:T(8,128)(2,1)S(1)}, bf16[1536,640]{1,0:T(8,128)(2,1)}, u32[]{:S(2)}) copy-start(bf16[1536,640]{1,0:T(8,128)(2,1)} %q_ref.3) | copy-start | bytes 5898244
  2.2 1.0 %copy-start.2 = (bf16[1536,128]{1,0:T(8,128)(2,1)S(1)}, bf16[1536,128]{1,0:T(8,128)(2,1)}, u32[]{:S(2)}) copy-start(bf16[1536,128]{1,0:T(8,128)(2,1)} %k_ref.3) | copy-start | bytes 1179652
  3.2 5.4 %copy-start.9 = (f32[640]{0:T(1024)S(1)}, f32[640]{0:T(1024)}, u32[]{:S(2)}) copy-start(f32[640]{0:T(1024)} %param.13) | copy-start | bytes 7684
  3.2 5.4 %copy-start.1 = (bf16[1536,640]{1,0:T(8,128)(2,1)S(1)}, bf16[1536,640]{1,0:T(8,128)(2,1)}, u32[]{:S(2)}) copy-start(bf16[1536,640]{1,0:T(8,128)(2,1)} %q_ref.3) | copy-start | bytes 5898244
  3.2 5.4 %copy-start.3 = (bf16[1536,128]{1,0:T(8,128)(2,1)S(1)}, bf16[1536,128]{1,0:T(8,128)(2,1)}, u32[]{:S(2)}) copy-start(bf16[1536,128]{1,0:T(8,128)(2,1)} %k_ref.3) | copy-start | bytes 1179652
  3.2 5.4 %copy-start.4 = (f32[128]{0:T(128)S(1)}, f32[128]{0:T(128)}, u32[]{:S(2)}) copy-start(f32[128]{0:T(128)} %param.14) | copy-start | bytes 1540
  3.2 5.4 %copy-start.6 = (s32[1,8]{1,0:T(1,128)S(1)}, s32[1,8]{1,0:T(1,128)}, u32[]{:S(2)}) copy-start(s32[1,8]{1,0:T(1,128)} %len_ref.1) | copy-start | bytes 100
  3.2 5.4 %copy-start.7 = (s32[1,8]{1,0:T(1,128)S(1)}, s32[1,8]{1,0:T(1,128)}, u32[]{:S(2)}) copy-start(s32[1,8]{1,0:T(1,128)} %dest_ref.1) | copy-start | bytes 100
  3.2 5.4 %copy-start.8 = (s32[1,8]{1,0:T(1,128)S(1)}, s32[1,8]{1,0:T(1,128)}, u32[]{:S(2)}) copy-start(s32[1,8]{1,0:T(1,128)} %off_ref.1) | copy-start | bytes 100
  8.6 1.0 %copy-start.5 = (bf16[1536,128]{1,0:T(8,128)(2,1)S(1)}, bf16[1536,128]{1,0:T(8,128)(2,1)}, u32[]{:S(2)}) copy-start(bf16[1536,128]{1,0:T(8,128)(2,1)} %v_ref.1) | copy-start | bytes 1179652

commit v3 on v2

--- a/solution.py
+++ b/solution.py
@@ -11,6 +11,8 @@
 HDIM = 128
 ROWS = 128
 REACH = 384
+CHUNKS = 4
+STEP_BLOCKS = 3
 
 eps = 1e-06
 big_negative = -1e30
@@ -40,8 +42,7 @@
     grad_ref,
     k_ref,
     v_ref,
-    recip_q_ref,
-    recip_k_ref,
+    recip_ref,
     q_gain_ref,
     k_gain_ref,
     dq_ref,
@@ -72,76 +73,100 @@
             at = slice(b * ROWS, (b + 1) * ROWS)
             normed = (
                 k_ref[at, :].astype(jnp.float32)
-                * column(recip_k_ref[b : b + 1, :])
+                * column(recip_ref[blocks + b : blocks + b + 1, :])
                 * k_gain_ref[...]
             )
             low = normed.astype(jnp.bfloat16)
             kn_ref[at, :] = low
             kn_t_ref[:, at] = jnp.transpose(low.astype(jnp.float32)).astype(jnp.bfloat16)
 
-    base = step * ROWS
-    token = base + lax.broadcasted_iota(jnp.int32, (1, ROWS), 1)
-    start = jnp.zeros((1, ROWS), jnp.int32)
-    first = jnp.int32(0)
-    end = jnp.int32(0)
-    for j in range(docs):
-        end = end + len_ref[0, j]
-        start = jnp.where(token >= end, end, start)
-        first = jnp.where(base >= end, end, first)
-    needed = step - first // ROWS + 1
-
-    def block(count):
+    def block(index, start, token, count):
         width = count * ROWS
-        key_at = pl.multiple_of((step - (count - 1)) * ROWS, ROWS)
+        key_at = pl.multiple_of((index - (count - 1)) * ROWS, ROWS)
         window = pl.ds(key_at, width)
-        recip = column(recip_q_ref[pl.ds(step, 1), :])
-        normed, upstream = [], []
-        for h in range(heads):
-            lanes = slice(h * HDIM, (h + 1) * HDIM)
-            tile = q_ref[:, lanes].astype(jnp.float32) * recip * q_gain_ref[:, lanes]
-            normed.append(tile.astype(jnp.bfloat16))
-            upstream.append(grad_ref[:, lanes])
-        queries = jnp.concatenate(normed, axis=0)
-        grads = jnp.concatenate(upstream, axis=0)
-        scores = nt_dot(kn_ref[window, :], queries)
-        grad_weights = nt_dot(v_ref[window, :], grads)
+        here_at = pl.multiple_of(index * ROWS, ROWS)
+        mine = pl.ds(pl.multiple_of(lax.rem(index, STEP_BLOCKS) * ROWS, ROWS), ROWS)
+        recip = column(recip_ref[pl.ds(index, 1), :])
         key = key_at + lax.broadcasted_iota(jnp.int32, (width, ROWS), 0)
         bias = jnp.where((key >= start) & (key <= token), 0.0, big_negative)
-        weights_all, grad_all = [], []
-        for h in range(heads):
-            lanes = slice(h * HDIM, (h + 1) * HDIM)
-            logits = scores[:, lanes] * (scaling * math.log2(math.e)) + bias
-            peak = jnp.max(logits, axis=0, keepdims=True)
-            powers = jnp.exp2(logits - peak)
-            total = jnp.sum(powers, axis=0, keepdims=True)
-            lse_ref[h : h + 1, pl.ds(pl.multiple_of(base, ROWS), ROWS)] = (
-                peak * math.log(2.0) + jnp.log(total)
-            )
-            weights = powers * (1.0 / total)
-            low = weights.astype(jnp.bfloat16)
-            upper = grad_weights[:, lanes]
-            delta = jnp.sum(low.astype(jnp.float32) * upper, axis=0, keepdims=True)
-            weights_all.append(low)
-            grad_all.append((weights * (upper - delta) * scaling).astype(jnp.bfloat16))
-        weights_low = jnp.concatenate(weights_all, axis=1)
-        grad_low = jnp.concatenate(grad_all, axis=1)
-        dv_acc[window, :] += jnp.dot(weights_low, grads, preferred_element_type=jnp.float32)
-        dk_acc[window, :] += jnp.dot(grad_low, queries, preferred_element_type=jnp.float32)
-        dq_t = jnp.dot(kn_t_ref[:, window], grad_low, preferred_element_type=jnp.float32)
-        inner = jnp.zeros((ROWS, HDIM), jnp.float32)
-        for h in range(heads):
-            lanes = slice(h * HDIM, (h + 1) * HDIM)
-            low = jnp.transpose(dq_t[:, lanes]).astype(jnp.bfloat16)
-            dq_ref[:, lanes] = low
-            inner += low.astype(jnp.float32) * q_gain_ref[:, lanes] * q_ref[:, lanes].astype(
-                jnp.float32
-            )
-        back_ref[pl.ds(step, 1), :] = row_sums(inner)
-
-    for count in range(1, REACH // ROWS + 2):
-        pl.when(needed == count)(functools.partial(block, count))
-
-    @pl.when(step == blocks - 1)
+        keys = kn_ref[window, :]
+        values = v_ref[window, :]
+        keys_t = kn_t_ref[:, window]
+
+        def products(group):
+            normed, upstream = [], []
+            for h in group:
+                lanes = slice(h * HDIM, (h + 1) * HDIM)
+                tile = q_ref[mine, lanes].astype(jnp.float32) * recip * q_gain_ref[:, lanes]
+                normed.append(tile.astype(jnp.bfloat16))
+                upstream.append(grad_ref[mine, lanes])
+            queries = jnp.concatenate(normed, axis=0)
+            grads = jnp.concatenate(upstream, axis=0)
+            return queries, grads, nt_dot(keys, queries), nt_dot(values, grads)
+
+        def softmax(group, scores, grad_weights):
+            weights_all, grad_all = [], []
+            for n, h in enumerate(group):
+                lanes = slice(n * HDIM, (n + 1) * HDIM)
+                logits = scores[:, lanes] * (scaling * math.log2(math.e)) + bias
+                peak = jnp.max(logits, axis=0, keepdims=True)
+                powers = jnp.exp2(logits - peak)
+                total = jnp.sum(powers, axis=0, keepdims=True)
+                lse_ref[h : h + 1, pl.ds(here_at, ROWS)] = peak * math.log(2.0) + jnp.log(total)
+                weights = powers * (1.0 / total)
+                low = weights.astype(jnp.bfloat16)
+                upper = grad_weights[:, lanes]
+                delta = jnp.sum(low.astype(jnp.float32) * upper, axis=0, keepdims=True)
+                weights_all.append(low)
+                grad_all.append((weights * (upper - delta) * scaling).astype(jnp.bfloat16))
+            return jnp.concatenate(weights_all, axis=1), jnp.concatenate(grad_all, axis=1)
+
+        def gradients(group, queries, grads, weights_low, grad_low):
+            dv = jnp.dot(weights_low, grads, preferred_element_type=jnp.float32)
+            dk = jnp.dot(grad_low, queries, preferred_element_type=jnp.float32)
+            dq_t = jnp.dot(keys_t, grad_low, preferred_element_type=jnp.float32)
+            inner = jnp.zeros((ROWS, HDIM), jnp.float32)
+            for n, h in enumerate(group):
+                lanes = slice(h * HDIM, (h + 1) * HDIM)
+                low = jnp.transpose(dq_t[:, n * HDIM : (n + 1) * HDIM]).astype(jnp.bfloat16)
+                dq_ref[mine, lanes] = low
+                inner += (
+                    low.astype(jnp.float32)
+                    * q_gain_ref[:, lanes]
+                    * q_ref[mine, lanes].astype(jnp.float32)
+                )
+            return dv, dk, inner
+
+        groups = [range(h, min(h + 2, heads)) for h in range(0, heads, 2)]
+        ready = [products(groups[0])]
+        results = []
+        for n, group in enumerate(groups):
+            if n + 1 < len(groups):
+                ready.append(products(groups[n + 1]))
+            queries, grads, scores, grad_weights = ready[n]
+            weights_low, grad_low = softmax(group, scores, grad_weights)
+            results.append(gradients(group, queries, grads, weights_low, grad_low))
+        dv_acc[window, :] += sum(r[0] for r in results)
+        dk_acc[window, :] += sum(r[1] for r in results)
+        back_ref[pl.ds(index, 1), :] = row_sums(sum(r[2] for r in results))
+
+    @pl.loop(0, STEP_BLOCKS)
+    def _(part):
+        index = step * STEP_BLOCKS + part
+        base = index * ROWS
+        token = base + lax.broadcasted_iota(jnp.int32, (1, ROWS), 1)
+        start = jnp.zeros((1, ROWS), jnp.int32)
+        first = jnp.int32(0)
+        end = jnp.int32(0)
+        for j in range(docs):
+            end = end + len_ref[0, j]
+            start = jnp.where(token >= end, end, start)
+            first = jnp.where(base >= end, end, first)
+        needed = index - first // ROWS + 1
+        for count in range(1, REACH // ROWS + 2):
+            pl.when(needed == count)(functools.partial(block, index, start, token, count))
+
+    @pl.when(step == pl.num_programs(0) - 1)
     def _():
         dv_ref[...] = dv_acc[...].astype(jnp.bfloat16)
         for b in range(blocks):
@@ -176,7 +201,7 @@
         home_ref[...] = home
 
 
-def attention(q, k, v, d_out, recip_q, recip_k, q_gain, k_gain, lengths, dest, offset, devices, slot):
+def attention(q, k, v, d_out, recip, q_gain, k_gain, lengths, dest, offset, devices, slot):
     seq_len, width = q.shape
     blocks = seq_len // ROWS
     home_count = seq_len // 4
@@ -185,11 +210,11 @@
     def whole(shape):
         return pl.BlockSpec(shape, lambda i: (0,) * len(shape))
 
-    rows = pl.BlockSpec((ROWS, width), lambda i: (i, 0))
+    rows = pl.BlockSpec((ROWS * STEP_BLOCKS, width), lambda i: (i, 0))
     kv = whole((seq_len, HDIM))
     return pl.pallas_call(
         functools.partial(attention_kernel, lengths.shape[1], devices, slot, home_count),
-        grid=(blocks,),
+        grid=(blocks // STEP_BLOCKS,),
         in_specs=[
             smem,
             smem,
@@ -198,8 +223,7 @@
             rows,
             kv,
             kv,
-            whole((blocks, ROWS)),
-            whole((blocks, ROWS)),
+            whole((2 * blocks, ROWS)),
             whole((1, width)),
             whole((1, HDIM)),
         ],
@@ -234,7 +258,7 @@
             bytes_accessed=8 * seq_len * width,
             transcendentals=seq_len * REACH * width // HDIM,
         ),
-    )(lengths, dest, offset, q, d_out, k, v, recip_q, recip_k, q_gain, k_gain)
+    )(lengths, dest, offset, q, d_out, k, v, recip, q_gain, k_gain)
 
 
 def peer_sum(parts_ref, got_ref, send_sem, recv_sem, me, peers):
@@ -253,10 +277,19 @@
     return copies
 
 
-def stat_kernel(peers, q_ref, k_ref, recip_ref, parts_ref, got_ref, send_sem, recv_sem):
+def stat_kernel(
+    peers, q_hbm, k_hbm, recip_ref, q_ref, k_ref, parts_ref, got_ref, send_sem, recv_sem, load_sem
+):
     me = lax.axis_index("head")
     seq_len, width = q_ref.shape
     blocks = seq_len // ROWS
+    part = seq_len // CHUNKS
+    loads = [pltpu.make_async_copy(k_hbm, k_ref, load_sem.at[CHUNKS])]
+    for c in range(CHUNKS):
+        at = pl.ds(c * part, part)
+        loads.append(pltpu.make_async_copy(q_hbm.at[at], q_ref.at[at], load_sem.at[c]))
+    for load in loads:
+        load.start()
     barrier = pltpu.get_barrier_semaphore()
     for d in range(1, peers):
         pl.semaphore_signal(
@@ -265,15 +298,20 @@
             device_id={"head": lax.rem(me + d, peers)},
             device_id_type=pl.DeviceIdType.MESH,
         )
+    loads[0].wait()
     for b in range(blocks):
+        at = slice(b * ROWS, (b + 1) * ROWS)
+        tile = k_ref[at, :].astype(jnp.float32)
+        parts_ref[blocks + b : blocks + b + 1, :] = row_sums(tile * tile)
+    for b in range(blocks):
+        if b % (blocks // CHUNKS) == 0:
+            loads[1 + b // (blocks // CHUNKS)].wait()
         at = slice(b * ROWS, (b + 1) * ROWS)
         total = jnp.zeros((ROWS, HDIM), jnp.float32)
         for h in range(width // HDIM):
             tile = q_ref[at, h * HDIM : (h + 1) * HDIM].astype(jnp.float32)
             total += tile * tile
         parts_ref[b : b + 1, :] = row_sums(total)
-        tile = k_ref[at, :].astype(jnp.float32)
-        parts_ref[blocks + b : blocks + b + 1, :] = row_sums(tile * tile)
     pl.semaphore_wait(barrier, peers - 1)
     copies = peer_sum(parts_ref, got_ref, send_sem, recv_sem, me, peers)
     for copy in copies:
@@ -291,13 +329,16 @@
     return pl.pallas_call(
         functools.partial(stat_kernel, peers),
         out_shape=jax.ShapeDtypeStruct((2 * blocks, ROWS), jnp.float32),
-        in_specs=[vmem, vmem],
+        in_specs=[pl.BlockSpec(memory_space=pl.ANY)] * 2,
         out_specs=vmem,
         scratch_shapes=[
+            pltpu.VMEM(q.shape, q.dtype),
+            pltpu.VMEM(k.shape, k.dtype),
             pltpu.VMEM((2 * blocks, ROWS), jnp.float32),
             pltpu.VMEM((peers - 1, 2 * blocks, ROWS), jnp.float32),
             pltpu.SemaphoreType.DMA((peers - 1,)),
             pltpu.SemaphoreType.DMA((peers - 1,)),
+            pltpu.SemaphoreType.DMA((CHUNKS + 1,)),
         ],
         compiler_params=pltpu.CompilerParams(
             collective_id=0, has_side_effects=True, vmem_limit_bytes=32 * 1024 * 1024
@@ -409,8 +450,7 @@
         k_raw,
         v_proj,
         d_out,
-        recip[:blocks],
-        recip[blocks:],
+        recip,
         q_gain.reshape(1, -1),
         k_gain.reshape(1, -1),
         doc_lengths,

time: 39.9 us -> 42.1 us (1.055); the launches traced: 40.2 us -> 41.7 us
  Pallas kernels: 31.9 us -> 32.7 us
  local copies, waits for them, and re-layouts: 3.57 us -> 4.28 us
    pallas_call x1, Pallas kernels: 5.3 us -> 7.18 us  [token_scales(): pl.pallas_call(functools.partial(stat_kernel, peers), out_shape=jax.Shape...]
    pallas_call x1, Pallas kernels: 8.56 us -> 7.58 us  [finish(): pl.pallas_call(functools.partial(finish_kernel, peers, devices, width * p...]
    reshape x1, local copies, waits for them, and re-layouts: 0.01 us -> 0.71 us  [local(): q_gain.reshape(1, -1)]
where the time goes in v3:
time: 42.1 us; the launch traced here: 41.7 us
  Pallas kernels  32.7 us (78%)
  local copies, waits for them, and re-layouts  4.28 us (10%)
  other arithmetic  3.93 us (9%)
  between operations  0.74 us (2%)
    pallas_call x1, Pallas kernels, attention(): pl.pallas_call(functools.partial(attention_kernel, lengths.shape[1], devi...  17.9 us
    pallas_call x1, Pallas kernels, finish(): pl.pallas_call(functools.partial(finish_kernel, peers, devices, width * p...  7.58 us
    pallas_call x1, Pallas kernels, token_scales(): pl.pallas_call(functools.partial(stat_kernel, peers), out_shape=jax.Shape...  7.18 us
    unnamed x20, local copies, waits for them, and re-layouts  3.56 us
    convert_element_type x1, other arithmetic, local(): (recip[0][:, None] * scaled_q - q_float * cubes[0][:, None]).astype(jnp.b...  2.05 us
    convert_element_type x1, other arithmetic, local(): (recip[1][:, None] * scaled_k - k_float * cubes[1][:, None]).astype(jnp.b...  1.22 us

profile of v3, /device:TPU:0, one launch (start us, length us, event | category | flops | bytes accessed | tf_op | source)
XLA Modules:
  0.0 41.7 jit_solution(3777443464672235285)
XLA Ops:
  0.6 0.0 copy-start.4
  0.6 0.0 copy-start.8
  0.7 0.0 copy-start.7
  0.7 0.0 copy-start.6
  0.7 0.7 %reshape.33.q_gain_ref = f32[1,640]{1,0:T(1,128)S(1)} reshape(f32[640]{0:T(1024)} %param.13) | data formatting | bytes 5120 | tf_op jit(solution)/shard_map/reshape | solution.py:454
  1.4 0.0 copy-start
  1.4 1.5 %copy-done = bf16[1536,640]{1,0:T(8,128)(2,1)S(1)} copy-done((bf16[1536,640]{1,0:T(8,128)(2,1)S(1)}, bf16[1536,640]{1,0:T(8,128)(2,1)}, u32[]{:S(2)}) %copy-start) | copy-done | bytes 1966104
  2.9 0.0 copy-start.2
  2.9 1.0 %copy-done.2 = bf16[1536,128]{1,0:T(8,128)(2,1)S(1)} copy-done((bf16[1536,128]{1,0:T(8,128)(2,1)S(1)}, bf16[1536,128]{1,0:T(8,128)(2,1)}, u32[]{:S(2)}) %copy-start.2) | copy-done | bytes 393240
  3.9 7.2 %shard_map.120.recip_ref = f32[24,128]{1,0:T(8,128)S(1)} custom-call(bf16[1536,640]{1,0:T(8,128)(2,1)S(1)} %copy-done, bf16[1536,128]{1,0:T(8,128)(2,1)S(1)} %copy-done.2), custom_call_target="tpu_custom_call" | custom-call | tf_op jit(solution)/shard_map/pallas_call | solution.py:329
  11.1 0.0 copy-done.4
  11.1 0.0 copy-done.8
  11.1 0.0 copy-done.7
  11.2 0.0 copy-done.6
  11.2 0.0 copy-done.1
  11.2 0.0 copy-done.3
  11.2 0.0 copy-start.5
  11.2 1.0 %copy-done.5 = bf16[1536,128]{1,0:T(8,128)(2,1)S(1)} copy-done((bf16[1536,128]{1,0:T(8,128)(2,1)S(1)}, bf16[1536,128]{1,0:T(8,128)(2,1)}, u32[]{:S(2)}) %copy-start.5) | copy-done | bytes 393240
  12.2 17.9 %shard_map.121 = (bf16[1536,640]{1,0:T(8,128)(2,1)S(1)}, bf16[1536,128]{1,0:T(8,128)(2,1)S(1)}, bf16[1536,128]{1,0:T(8,128)(2,1)}, f32[24,128]{1,0:T(8,128)S(1)}...) custom-call(s32[1,8]{1,0:T(1,128)S(1)} %copy-done.6, s32[1,8]{1,0:T(1,128)S(1)} %copy-done.7, s32[1,8]{1,0:T(1,128)S(1)} %copy-done.8, ...), custom_call_target="tpu_custom_call" | custom-call | flops 3774873600 | bytes 7864320 | tf_op jit(solution)/shard_map/pallas_call | solution.py:215
  30.1 7.6 %shard_map.122 = (f32[24,128]{1,0:T(8,128)S(1)}, f32[8,8,384]{2,1,0:T(8,128)S(1)}) custom-call(f32[24,128]{1,0:T(8,128)S(1)} %shard_map.120.recip_ref, f32[24,128]{1,0:T(8,128)S(1)} %get-tuple-element.13.back_ref, f32[8,8,384]{2,1,0:T(8,128)S(1)} %get-tuple-element.14.slots_ref), custom_call_target="tpu_custom_call" | custom-call | tf_op jit(solution)/shard_map/pallas_call | solution.py:417
  37.7 0.7 %pad_maximum_fusion = f32[5,3456]{1,0:T(8,128)} fusion(f32[5,3072]{1,0:T(8,128)S(1)} %bitcast.14, f32[5,384]{1,0:T(8,128)S(1)} %bitcast.15), kind=kLoop, calls=%fused_computation.2 | loop fusion | flops 17280 | bytes 138240 | tf_op jit(solution)/shard_map/concatenate | solution.py:464
  38.4 1.2 %subtract_convert_fusion.1 = bf16[1536,128]{1,0:T(8,128)(2,1)} fusion(bf16[1536,128]{1,0:T(8,128)(2,1)S(1)} %copy-done.3, bf16[1536,128]{1,0:T(8,128)(2,1)S(1)} %get-tuple-element.16, f32[1536]{0:T(1024)S(1)} %get-tuple-element.22, f32[128]{0:T(128)S(1)} %copy-done.4, f32[1536]{0:T(1024)S(1)} %get-tuple-element.25), kind=kLoop, calls=%fused_computation.1 | loop fusion | flops 1376256 | bytes 1192448 | tf_op jit(solution)/shard_map/convert_element_type | solution.py:472
  39.6 0.0 copy-done.9
  39.6 2.0 %subtract_convert_fusion = bf16[1536,640]{1,0:T(8,128)(2,1)} fusion(bf16[1536,640]{1,0:T(8,128)(2,1)S(1)} %copy-done.1, bf16[1536,640]{1,0:T(8,128)(2,1)S(1)} %get-tuple-element.12, f32[1536]{0:T(1024)S(1)} %get-tuple-element.23, f32[640]{0:T(1024)S(1)} %copy-done.9, f32[1536]{0:T(1024)S(1)} %get-tuple-element.24), kind=kLoop, calls=%fused_computation | loop fusion | flops 6881280 | bytes 5913088 | tf_op jit(solution)/shard_map/convert_element_type | solution.py:471
  (4 shorter events, 0.0 us)
Async XLA Ops:
  0.6 10.5 %copy-start.4 = (f32[128]{0:T(128)S(1)}, f32[128]{0:T(128)}, u32[]{:S(2)}) copy-start(f32[128]{0:T(128)} %param.14) | copy-start | bytes 1540
  0.6 10.5 %copy-start.8 = (s32[1,8]{1,0:T(1,128)S(1)}, s32[1,8]{1,0:T(1,128)}, u32[]{:S(2)}) copy-start(s32[1,8]{1,0:T(1,128)} %off_ref.1) | copy-start | bytes 100
  0.7 10.5 %copy-start.7 = (s32[1,8]{1,0:T(1,128)S(1)}, s32[1,8]{1,0:T(1,128)}, u32[]{:S(2)}) copy-start(s32[1,8]{1,0:T(1,128)} %dest_ref.1) | copy-start | bytes 100
  0.7 10.5 %copy-start.6 = (s32[1,8]{1,0:T(1,128)S(1)}, s32[1,8]{1,0:T(1,128)}, u32[]{:S(2)}) copy-start(s32[1,8]{1,0:T(1,128)} %len_ref.1) | copy-start | bytes 100
  1.4 1.5 %copy-start = (bf16[1536,640]{1,0:T(8,128)(2,1)S(1)}, bf16[1536,640]{1,0:T(8,128)(2,1)}, u32[]{:S(2)}) copy-start(bf16[1536,640]{1,0:T(8,128)(2,1)} %q_ref.1) | copy-start | bytes 5898244
  2.9 1.0 %copy-start.2 = (bf16[1536,128]{1,0:T(8,128)(2,1)S(1)}, bf16[1536,128]{1,0:T(8,128)(2,1)}, u32[]{:S(2)}) copy-start(bf16[1536,128]{1,0:T(8,128)(2,1)} %k_ref.1) | copy-start | bytes 1179652
  3.9 7.2 %copy-start.1 = (bf16[1536,640]{1,0:T(8,128)(2,1)S(1)}, bf16[1536,640]{1,0:T(8,128)(2,1)}, u32[]{:S(2)}) copy-start(bf16[1536,640]{1,0:T(8,128)(2,1)} %q_ref.1) | copy-start | bytes 5898244
  3.9 7.2 %copy-start.3 = (bf16[1536,128]{1,0:T(8,128)(2,1)S(1)}, bf16[1536,128]{1,0:T(8,128)(2,1)}, u32[]{:S(2)}) copy-start(bf16[1536,128]{1,0:T(8,128)(2,1)} %k_ref.1) | copy-start | bytes 1179652
  11.2 1.0 %copy-start.5 = (bf16[1536,128]{1,0:T(8,128)(2,1)S(1)}, bf16[1536,128]{1,0:T(8,128)(2,1)}, u32[]{:S(2)}) copy-start(bf16[1536,128]{1,0:T(8,128)(2,1)} %v_ref.1) | copy-start | bytes 1179652
  12.2 27.4 %copy-start.9 = (f32[640]{0:T(1024)S(1)}, f32[640]{0:T(1024)}, u32[]{:S(2)}) copy-start(f32[640]{0:T(1024)} %param.13) | copy-start | bytes 7684

commit v4 on v3

--- a/solution.py
+++ b/solution.py
@@ -12,7 +12,7 @@
 ROWS = 128
 REACH = 384
 CHUNKS = 4
-STEP_BLOCKS = 3
+TILE = 2
 
 eps = 1e-06
 big_negative = -1e30
@@ -41,7 +41,7 @@
     q_ref,
     grad_ref,
     k_ref,
-    v_ref,
+    v_hbm,
     recip_ref,
     q_gain_ref,
     k_gain_ref,
@@ -56,6 +56,8 @@
     dk_acc,
     dv_acc,
     lse_ref,
+    v_ref,
+    v_sem,
 ):
     step = pl.program_id(0)
     seq_len = k_ref.shape[0]
@@ -66,6 +68,8 @@
 
     @pl.when(step == 0)
     def _():
+        load = pltpu.make_async_copy(v_hbm, v_ref, v_sem)
+        load.start()
         dk_acc[...] = jnp.zeros_like(dk_acc)
         dv_acc[...] = jnp.zeros_like(dv_acc)
         lse_ref[...] = jnp.zeros_like(lse_ref)
@@ -79,92 +83,81 @@
             low = normed.astype(jnp.bfloat16)
             kn_ref[at, :] = low
             kn_t_ref[:, at] = jnp.transpose(low.astype(jnp.float32)).astype(jnp.bfloat16)
-
-    def block(index, start, token, count):
+        load.wait()
+
+    base = step * TILE * ROWS
+    token = base + lax.broadcasted_iota(jnp.int32, (1, TILE * ROWS), 1)
+    start = jnp.zeros((1, TILE * ROWS), jnp.int32)
+    first = jnp.int32(0)
+    end = jnp.int32(0)
+    for j in range(docs):
+        end = end + len_ref[0, j]
+        start = jnp.where(token >= end, end, start)
+        first = jnp.where(base >= end, end, first)
+    needed = step * TILE - first // ROWS + TILE
+
+    def block(count):
         width = count * ROWS
-        key_at = pl.multiple_of((index - (count - 1)) * ROWS, ROWS)
+        key_at = pl.multiple_of((step * TILE + TILE - count) * ROWS, ROWS)
         window = pl.ds(key_at, width)
-        here_at = pl.multiple_of(index * ROWS, ROWS)
-        mine = pl.ds(pl.multiple_of(lax.rem(index, STEP_BLOCKS) * ROWS, ROWS), ROWS)
-        recip = column(recip_ref[pl.ds(index, 1), :])
-        key = key_at + lax.broadcasted_iota(jnp.int32, (width, ROWS), 0)
+        mine = pl.ds(pl.multiple_of(base, TILE * ROWS), TILE * ROWS)
+        recip = jnp.concatenate(
+            [column(recip_ref[pl.ds(step * TILE + n, 1), :]) for n in range(TILE)], axis=0
+        )
+        key = key_at + lax.broadcasted_iota(jnp.int32, (width, TILE * ROWS), 0)
         bias = jnp.where((key >= start) & (key <= token), 0.0, big_negative)
         keys = kn_ref[window, :]
         values = v_ref[window, :]
         keys_t = kn_t_ref[:, window]
 
-        def products(group):
-            normed, upstream = [], []
-            for h in group:
-                lanes = slice(h * HDIM, (h + 1) * HDIM)
-                tile = q_ref[mine, lanes].astype(jnp.float32) * recip * q_gain_ref[:, lanes]
-                normed.append(tile.astype(jnp.bfloat16))
-                upstream.append(grad_ref[mine, lanes])
-            queries = jnp.concatenate(normed, axis=0)
-            grads = jnp.concatenate(upstream, axis=0)
+        def products(h):
+            lanes = slice(h * HDIM, (h + 1) * HDIM)
+            tile = q_ref[:, lanes].astype(jnp.float32) * recip * q_gain_ref[:, lanes]
+            queries = tile.astype(jnp.bfloat16)
+            grads = grad_ref[:, lanes]
             return queries, grads, nt_dot(keys, queries), nt_dot(values, grads)
 
-        def softmax(group, scores, grad_weights):
-            weights_all, grad_all = [], []
-            for n, h in enumerate(group):
-                lanes = slice(n * HDIM, (n + 1) * HDIM)
-                logits = scores[:, lanes] * (scaling * math.log2(math.e)) + bias
-                peak = jnp.max(logits, axis=0, keepdims=True)
-                powers = jnp.exp2(logits - peak)
-                total = jnp.sum(powers, axis=0, keepdims=True)
-                lse_ref[h : h + 1, pl.ds(here_at, ROWS)] = peak * math.log(2.0) + jnp.log(total)
-                weights = powers * (1.0 / total)
-                low = weights.astype(jnp.bfloat16)
-                upper = grad_weights[:, lanes]
-                delta = jnp.sum(low.astype(jnp.float32) * upper, axis=0, keepdims=True)
-                weights_all.append(low)
-                grad_all.append((weights * (upper - delta) * scaling).astype(jnp.bfloat16))
-            return jnp.concatenate(weights_all, axis=1), jnp.concatenate(grad_all, axis=1)
-
-        def gradients(group, queries, grads, weights_low, grad_low):
+        def softmax(h, scores, upper):
+            logits = scores * (scaling * math.log2(math.e)) + bias
+            peak = jnp.max(logits, axis=0, keepdims=True)
+            powers = jnp.exp2(logits - peak)
+            total = jnp.sum(powers, axis=0, keepdims=True)
+            lse_ref[h : h + 1, mine] = peak * math.log(2.0) + jnp.log(total)
+            weights = powers * (1.0 / total)
+            low = weights.astype(jnp.bfloat16)
+            delta = jnp.sum(low.astype(jnp.float32) * upper, axis=0, keepdims=True)
+            return low, (weights * (upper - delta) * scaling).astype(jnp.bfloat16)
+
+        def gradients(h, queries, grads, weights_low, grad_low):
+            lanes = slice(h * HDIM, (h + 1) * HDIM)
             dv = jnp.dot(weights_low, grads, preferred_element_type=jnp.float32)
             dk = jnp.dot(grad_low, queries, preferred_element_type=jnp.float32)
             dq_t = jnp.dot(keys_t, grad_low, preferred_element_type=jnp.float32)
-            inner = jnp.zeros((ROWS, HDIM), jnp.float32)
-            for n, h in enumerate(group):
-                lanes = slice(h * HDIM, (h + 1) * HDIM)
-                low = jnp.transpose(dq_t[:, n * HDIM : (n + 1) * HDIM]).astype(jnp.bfloat16)
-                dq_ref[mine, lanes] = low
-                inner += (
-                    low.astype(jnp.float32)
-                    * q_gain_ref[:, lanes]
-                    * q_ref[mine, lanes].astype(jnp.float32)
-                )
+            low = jnp.transpose(dq_t).astype(jnp.bfloat16)
+            dq_ref[:, lanes] = low
+            inner = (
+                low.astype(jnp.float32)
+                * q_gain_ref[:, lanes]
+                * q_ref[:, lanes].astype(jnp.float32)
+            )
             return dv, dk, inner
 
-        groups = [range(h, min(h + 2, heads)) for h in range(0, heads, 2)]
-        ready = [products(groups[0])]
-        results = []
-        for n, group in enumerate(groups):
-            if n + 1 < len(groups):
-                ready.append(products(groups[n + 1]))
-            queries, grads, scores, grad_weights = ready[n]
-            weights_low, grad_low = softmax(group, scores, grad_weights)
-            results.append(gradients(group, queries, grads, weights_low, grad_low))
-        dv_acc[window, :] += sum(r[0] for r in results)
-        dk_acc[window, :] += sum(r[1] for r in results)
-        back_ref[pl.ds(index, 1), :] = row_sums(sum(r[2] for r in results))
-
-    @pl.loop(0, STEP_BLOCKS)
-    def _(part):
-        index = step * STEP_BLOCKS + part
-        base = index * ROWS
-        token = base + lax.broadcasted_iota(jnp.int32, (1, ROWS), 1)
-        start = jnp.zeros((1, ROWS), jnp.int32)
-        first = jnp.int32(0)
-        end = jnp.int32(0)
-        for j in range(docs):
-            end = end + len_ref[0, j]
-            start = jnp.where(token >= end, end, start)
-            first = jnp.where(base >= end, end, first)
-        needed = index - first // ROWS + 1
-        for count in range(1, REACH // ROWS + 2):
-            pl.when(needed == count)(functools.partial(block, index, start, token, count))
+        ready = [products(0)]
+        inner = jnp.zeros((TILE * ROWS, HDIM), jnp.float32)
+        for h in range(heads):
+            if h + 1 < heads:
+                ready.append(products(h + 1))
+            queries, grads, scores, upper = ready[h]
+            weights_low, grad_low = softmax(h, scores, upper)
+            dv, dk, term = gradients(h, queries, grads, weights_low, grad_low)
+            dv_acc[window, :] += dv
+            dk_acc[window, :] += dk
+            inner += term
+        for n in range(TILE):
+            back_ref[pl.ds(step * TILE + n, 1), :] = row_sums(inner[n * ROWS : (n + 1) * ROWS])
+
+    for count in range(TILE, REACH // ROWS + TILE + 1):
+        pl.when(needed == count)(functools.partial(block, count))
 
     @pl.when(step == pl.num_programs(0) - 1)
     def _():
@@ -210,11 +203,11 @@
     def whole(shape):
         return pl.BlockSpec(shape, lambda i: (0,) * len(shape))
 
-    rows = pl.BlockSpec((ROWS * STEP_BLOCKS, width), lambda i: (i, 0))
+    rows = pl.BlockSpec((ROWS * TILE, width), lambda i: (i, 0))
     kv = whole((seq_len, HDIM))
     return pl.pallas_call(
         functools.partial(attention_kernel, lengths.shape[1], devices, slot, home_count),
-        grid=(blocks // STEP_BLOCKS,),
+        grid=(blocks // TILE,),
         in_specs=[
             smem,
             smem,
@@ -222,7 +215,7 @@
             rows,
             rows,
             kv,
-            kv,
+            pl.BlockSpec(memory_space=pltpu.HBM),
             whole((2 * blocks, ROWS)),
             whole((1, width)),
             whole((1, HDIM)),
@@ -249,9 +242,11 @@
             pltpu.VMEM((seq_len, HDIM), jnp.float32),
             pltpu.VMEM((seq_len, HDIM), jnp.float32),
             pltpu.VMEM((8, seq_len), jnp.float32),
+            pltpu.VMEM((seq_len, HDIM), jnp.bfloat16),
+            pltpu.SemaphoreType.DMA,
         ],
         compiler_params=pltpu.CompilerParams(
-            vmem_limit_bytes=48 * 1024 * 1024, dimension_semantics=("arbitrary",)
+            vmem_limit_bytes=61 * 1024 * 1024, dimension_semantics=("arbitrary",)
         ),
         cost_estimate=pl.CostEstimate(
             flops=10 * seq_len * REACH * width,
@@ -329,7 +324,7 @@
     return pl.pallas_call(
         functools.partial(stat_kernel, peers),
         out_shape=jax.ShapeDtypeStruct((2 * blocks, ROWS), jnp.float32),
-        in_specs=[pl.BlockSpec(memory_space=pl.ANY)] * 2,
+        in_specs=[pl.BlockSpec(memory_space=pltpu.HBM)] * 2,
         out_specs=vmem,
         scratch_shapes=[
             pltpu.VMEM(q.shape, q.dtype),
@@ -341,7 +336,7 @@
             pltpu.SemaphoreType.DMA((CHUNKS + 1,)),
         ],
         compiler_params=pltpu.CompilerParams(
-            collective_id=0, has_side_effects=True, vmem_limit_bytes=32 * 1024 * 1024
+            collective_id=0, has_side_effects=True, vmem_limit_bytes=63 * 1024 * 1024
         ),
     )(q, k)
 
@@ -350,8 +345,8 @@
     peers,
     devices,
     width_q,
-    recip_ref,
-    back_ref,
+    recip_hbm,
+    back_hbm,
     slots_ref,
     cube_ref,
     logs_ref,
@@ -361,11 +356,17 @@
     recv_sem,
     log_send_sem,
     log_recv_sem,
+    recip_ref,
+    back_ref,
+    load_sem,
 ):
     me = lax.axis_index("head")
     here = lax.axis_index("dp")
-    rows = back_ref.shape[0]
-    blocks = rows // 2
+    blocks = back_ref.shape[0] // 2
+    load_back = pltpu.make_async_copy(back_hbm, back_ref, load_sem.at[0])
+    load_recip = pltpu.make_async_copy(recip_hbm, recip_ref, load_sem.at[1])
+    load_back.start()
+    load_recip.start()
     barrier = pltpu.get_barrier_semaphore()
     for d in range(1, peers):
         pl.semaphore_signal(
@@ -381,6 +382,8 @@
             device_id={"dp": lax.rem(here + d, devices)},
             device_id_type=pl.DeviceIdType.MESH,
         )
+    load_back.wait()
+    load_recip.wait()
     pl.semaphore_wait(barrier, peers - 1 + devices - 1)
     copies = peer_sum(back_ref, got_ref, send_sem, recv_sem, me, peers)
     log_copies = []
@@ -420,7 +423,7 @@
             jax.ShapeDtypeStruct(back.shape, jnp.float32),
             jax.ShapeDtypeStruct(slots.shape, jnp.float32),
         ],
-        in_specs=[vmem, vmem, vmem],
+        in_specs=[pl.BlockSpec(memory_space=pl.ANY)] * 3,
         out_specs=[vmem, vmem],
         scratch_shapes=[
             pltpu.VMEM((peers - 1,) + back.shape, jnp.float32),
@@ -429,6 +432,9 @@
             pltpu.SemaphoreType.DMA((peers - 1,)),
             pltpu.SemaphoreType.DMA((devices - 1,)),
             pltpu.SemaphoreType.DMA((devices - 1,)),
+            pltpu.VMEM(back.shape, jnp.float32),
+            pltpu.VMEM(back.shape, jnp.float32),
+            pltpu.SemaphoreType.DMA((2,)),
         ],
         compiler_params=pltpu.CompilerParams(
             collective_id=1, has_side_effects=True, vmem_limit_bytes=32 * 1024 * 1024

time: 42.1 us -> 44.3 us (1.052)
  other arithmetic: 3.93 us -> 6.82 us
  local copies, waits for them, and re-layouts: 4.28 us -> 2.91 us
  Pallas kernels: 32.7 us -> 33.5 us
    unnamed x20 -> x14, local copies, waits for them, and re-layouts: 3.56 us -> 1.62 us
    convert_element_type x1, other arithmetic: 2.05 us -> 3.23 us  [local(): (recip[0][:, None] * scaled_q - q_float * cubes[0][:, None]).astype(jnp.b...]
    convert_element_type x1, other arithmetic: 1.22 us -> 2.22 us  [local(): (recip[1][:, None] * scaled_k - k_float * cubes[1][:, None]).astype(jnp.b...]
    pallas_call x1, Pallas kernels: 17.9 us -> 18.7 us  [attention(): pl.pallas_call(functools.partial(attention_kernel, lengths.shape[1], devi...]
    concatenate x1, other arithmetic: 0.66 us -> 1.36 us  [local(): balanced = jnp.concatenate([home_log[:heads], away_log], axis=1)]
    reshape x1, local copies, waits for them, and re-layouts: 0.71 us -> 1.28 us  [local(): q_gain.reshape(1, -1)]
where the time goes in v4:
time: 44.3 us; the launch traced here: 43.9 us
  Pallas kernels  33.5 us (76%)
  other arithmetic  6.82 us (15%)
  local copies, waits for them, and re-layouts  2.91 us (7%)
  between operations  0.72 us (2%)
    pallas_call x1, Pallas kernels, attention(): pl.pallas_call(functools.partial(attention_kernel, lengths.shape[1], devi...  18.7 us
    pallas_call x1, Pallas kernels, finish(): pl.pallas_call(functools.partial(finish_kernel, peers, devices, width * p...  7.44 us
    pallas_call x1, Pallas kernels, token_scales(): pl.pallas_call(functools.partial(stat_kernel, peers), out_shape=jax.Shape...  7.31 us
    convert_element_type x1, other arithmetic, local(): (recip[0][:, None] * scaled_q - q_float * cubes[0][:, None]).astype(jnp.b...  3.23 us
    convert_element_type x1, other arithmetic, local(): (recip[1][:, None] * scaled_k - k_float * cubes[1][:, None]).astype(jnp.b...  2.22 us
    unnamed x14, local copies, waits for them, and re-layouts  1.62 us
    concatenate x1, other arithmetic, local(): balanced = jnp.concatenate([home_log[:heads], away_log], axis=1)  1.36 us
    reshape x1, local copies, waits for them, and re-layouts, local(): q_gain.reshape(1, -1)  1.28 us

profile of v4, /device:TPU:0, one launch (start us, length us, event | category | flops | bytes accessed | tf_op | source)
XLA Modules:
  0.0 43.9 jit_solution(18191681112593557019)
XLA Ops:
  0.6 1.3 %reshape.33.q_gain_ref = f32[1,640]{1,0:T(1,128)} reshape(f32[640]{0:T(1024)} %param.13) | data formatting | bytes 5120 | tf_op jit(solution)/shard_map/reshape | solution.py:460
  1.9 7.3 %shard_map.120.recip_ref.recip_hbm = f32[24,128]{1,0:T(8,128)} custom-call(bf16[1536,640]{1,0:T(8,128)(2,1)} %q_ref.1, bf16[1536,128]{1,0:T(8,128)(2,1)} %k_ref.1), custom_call_target="tpu_custom_call" | custom-call | tf_op jit(solution)/shard_map/pallas_call | solution.py:324
  9.2 0.0 copy-start
  9.2 0.0 copy-start.4
  9.2 0.0 copy-start.6
  9.3 0.0 copy-start.3
  9.3 0.0 copy-start.5
  9.3 18.7 %shard_map.121 = (bf16[1536,640]{1,0:T(8,128)(2,1)}, bf16[1536,128]{1,0:T(8,128)(2,1)}, bf16[1536,128]{1,0:T(8,128)(2,1)}, f32[24,128]{1,0:T(8,128)}, f32[8,384]{1,0:T(8,128)}, /*index=5*/f32[8,8,384]{2,1,0:T(8,128)}) custom-call(s32[1,8]{1,0:T(1,128)} %len_ref.1, s32[1,8]{1,0:T(1,128)} %dest_ref.1, s32[1,8]{1,0:T(1,128)} %off_ref.1, ...), custom_call_target="tpu_custom_call" | custom-call | flops 3774873600 | bytes 7864320 | tf_op jit(solution)/shard_map/pallas_call | solution.py:208
  28.0 0.0 copy-done
  28.0 0.0 copy-start.1
  28.1 0.9 %copy-done.1 = f32[8,8,384]{2,1,0:T(8,128)S(1)} copy-done((f32[8,8,384]{2,1,0:T(8,128)S(1)}, f32[8,8,384]{2,1,0:T(8,128)}, u32[]{:S(2)}) %copy-start.1) | copy-done | bytes 98328
  28.9 0.0 copy-start.2
  28.9 0.7 %copy-done.2 = f32[24,128]{1,0:T(8,128)S(1)} copy-done((f32[24,128]{1,0:T(8,128)S(1)}, f32[24,128]{1,0:T(8,128)}, u32[]{:S(2)}) %copy-start.2) | copy-done | bytes 12312
  29.7 7.4 %shard_map.122 = (f32[24,128]{1,0:T(8,128)S(1)}, f32[8,8,384]{2,1,0:T(8,128)S(1)}) custom-call(f32[24,128]{1,0:T(8,128)S(1)} %copy-done, f32[24,128]{1,0:T(8,128)S(1)} %copy-done.2, f32[8,8,384]{2,1,0:T(8,128)S(1)} %copy-done.1), custom_call_target="tpu_custom_call" | custom-call | tf_op jit(solution)/shard_map/pallas_call | solution.py:420
  37.1 1.4 %pad_maximum_fusion = f32[5,3456]{1,0:T(8,128)} fusion(f32[5,3072]{1,0:T(8,128)S(1)} %bitcast.14, f32[5,384]{1,0:T(8,128)} %bitcast.15), kind=kLoop, calls=%fused_computation.2 | loop fusion | flops 17280 | bytes 138240 | tf_op jit(solution)/shard_map/concatenate | solution.py:470
  38.5 0.0 copy-done.4
  38.5 0.0 copy-done.6
  38.5 2.2 %subtract_convert_fusion.1 = bf16[1536,128]{1,0:T(8,128)(2,1)} fusion(bf16[1536,128]{1,0:T(8,128)(2,1)S(1)} %copy-done.4, bf16[1536,128]{1,0:T(8,128)(2,1)} %get-tuple-element.16, f32[1536]{0:T(1024)S(1)} %get-tuple-element.22, f32[128]{0:T(128)S(1)} %copy-done.6, f32[1536]{0:T(1024)S(1)} %get-tuple-element.25), kind=kLoop, calls=%fused_computation.1 | loop fusion | flops 1376256 | bytes 1192448 | tf_op jit(solution)/shard_map/convert_element_type | solution.py:478
  40.7 0.0 copy-done.3
  40.7 0.0 copy-done.5
  40.7 3.2 %subtract_convert_fusion = bf16[1536,640]{1,0:T(8,128)(2,1)} fusion(bf16[1536,640]{1,0:T(8,128)(2,1)S(1)} %copy-done.3, bf16[1536,640]{1,0:T(8,128)(2,1)} %get-tuple-element.12, f32[1536]{0:T(1024)S(1)} %get-tuple-element.23, f32[640]{0:T(1024)S(1)} %copy-done.5, f32[1536]{0:T(1024)S(1)} %get-tuple-element.24), kind=kLoop, calls=%fused_computation | loop fusion | flops 6881280 | bytes 5913088 | tf_op jit(solution)/shard_map/convert_element_type | solution.py:477
  (1 shorter events, 0.0 us)
Async XLA Ops:
  9.2 18.8 %copy-start = (f32[24,128]{1,0:T(8,128)S(1)}, f32[24,128]{1,0:T(8,128)}, u32[]{:S(2)}) copy-start(f32[24,128]{1,0:T(8,128)} %shard_map.120.recip_ref.recip_hbm) | copy-start | bytes 36868
  9.2 29.2 %copy-start.4 = (bf16[1536,128]{1,0:T(8,128)(2,1)S(1)}, bf16[1536,128]{1,0:T(8,128)(2,1)}, u32[]{:S(2)}) copy-start(bf16[1536,128]{1,0:T(8,128)(2,1)} %k_ref.1) | copy-start | bytes 1179652
  9.2 29.2 %copy-start.6 = (f32[128]{0:T(128)S(1)}, f32[128]{0:T(128)}, u32[]{:S(2)}) copy-start(f32[128]{0:T(128)} %param.14) | copy-start | bytes 1540
  9.3 31.4 %copy-start.3 = (bf16[1536,640]{1,0:T(8,128)(2,1)S(1)}, bf16[1536,640]{1,0:T(8,128)(2,1)}, u32[]{:S(2)}) copy-start(bf16[1536,640]{1,0:T(8,128)(2,1)} %q_ref.1) | copy-start | bytes 5898244
  9.3 31.4 %copy-start.5 = (f32[640]{0:T(1024)S(1)}, f32[640]{0:T(1024)}, u32[]{:S(2)}) copy-start(f32[640]{0:T(1024)} %param.13) | copy-start | bytes 7684
  28.0 0.9 %copy-start.1 = (f32[8,8,384]{2,1,0:T(8,128)S(1)}, f32[8,8,384]{2,1,0:T(8,128)}, u32[]{:S(2)}) copy-start(f32[8,8,384]{2,1,0:T(8,128)} %get-tuple-element.14.slots_ref) | copy-start | bytes 294916
  28.9 0.7 %copy-start.2 = (f32[24,128]{1,0:T(8,128)S(1)}, f32[24,128]{1,0:T(8,128)}, u32[]{:S(2)}) copy-start(f32[24,128]{1,0:T(8,128)} %get-tuple-element.13.back_hbm) | copy-start | bytes 36868

commit v5 on v3

--- a/solution.py
+++ b/solution.py
@@ -11,7 +11,6 @@
 HDIM = 128
 ROWS = 128
 REACH = 384
-CHUNKS = 4
 STEP_BLOCKS = 3
 
 eps = 1e-06
@@ -277,19 +276,10 @@
     return copies
 
 
-def stat_kernel(
-    peers, q_hbm, k_hbm, recip_ref, q_ref, k_ref, parts_ref, got_ref, send_sem, recv_sem, load_sem
-):
+def stat_kernel(peers, q_ref, k_ref, recip_ref, parts_ref, got_ref, send_sem, recv_sem):
     me = lax.axis_index("head")
     seq_len, width = q_ref.shape
     blocks = seq_len // ROWS
-    part = seq_len // CHUNKS
-    loads = [pltpu.make_async_copy(k_hbm, k_ref, load_sem.at[CHUNKS])]
-    for c in range(CHUNKS):
-        at = pl.ds(c * part, part)
-        loads.append(pltpu.make_async_copy(q_hbm.at[at], q_ref.at[at], load_sem.at[c]))
-    for load in loads:
-        load.start()
     barrier = pltpu.get_barrier_semaphore()
     for d in range(1, peers):
         pl.semaphore_signal(
@@ -298,20 +288,15 @@
             device_id={"head": lax.rem(me + d, peers)},
             device_id_type=pl.DeviceIdType.MESH,
         )
-    loads[0].wait()
     for b in range(blocks):
-        at = slice(b * ROWS, (b + 1) * ROWS)
-        tile = k_ref[at, :].astype(jnp.float32)
-        parts_ref[blocks + b : blocks + b + 1, :] = row_sums(tile * tile)
-    for b in range(blocks):
-        if b % (blocks // CHUNKS) == 0:
-            loads[1 + b // (blocks // CHUNKS)].wait()
         at = slice(b * ROWS, (b + 1) * ROWS)
         total = jnp.zeros((ROWS, HDIM), jnp.float32)
         for h in range(width // HDIM):
             tile = q_ref[at, h * HDIM : (h + 1) * HDIM].astype(jnp.float32)
             total += tile * tile
         parts_ref[b : b + 1, :] = row_sums(total)
+        tile = k_ref[at, :].astype(jnp.float32)
+        parts_ref[blocks + b : blocks + b + 1, :] = row_sums(tile * tile)
     pl.semaphore_wait(barrier, peers - 1)
     copies = peer_sum(parts_ref, got_ref, send_sem, recv_sem, me, peers)
     for copy in copies:
@@ -329,16 +314,13 @@
     return pl.pallas_call(
         functools.partial(stat_kernel, peers),
         out_shape=jax.ShapeDtypeStruct((2 * blocks, ROWS), jnp.float32),
-        in_specs=[pl.BlockSpec(memory_space=pl.ANY)] * 2,
+        in_specs=[vmem, vmem],
         out_specs=vmem,
         scratch_shapes=[
-            pltpu.VMEM(q.shape, q.dtype),
-            pltpu.VMEM(k.shape, k.dtype),
             pltpu.VMEM((2 * blocks, ROWS), jnp.float32),
             pltpu.VMEM((peers - 1, 2 * blocks, ROWS), jnp.float32),
             pltpu.SemaphoreType.DMA((peers - 1,)),
             pltpu.SemaphoreType.DMA((peers - 1,)),
-            pltpu.SemaphoreType.DMA((CHUNKS + 1,)),
         ],
         compiler_params=pltpu.CompilerParams(
             collective_id=0, has_side_effects=True, vmem_limit_bytes=32 * 1024 * 1024

time: 42.1 us -> 40.1 us (0.952)
  Pallas kernels: 32.7 us -> 30.3 us
    pallas_call x1, Pallas kernels: 7.18 us -> 5.25 us  [token_scales(): pl.pallas_call(functools.partial(stat_kernel, peers), out_shape=jax.Shape...]
    pallas_call x1, Pallas kernels: 17.9 us -> 17.3 us  [attention(): pl.pallas_call(functools.partial(attention_kernel, lengths.shape[1], devi...]
where the time goes in v5:
time: 40.1 us; the launch traced here: 39.3 us
  Pallas kernels  30.3 us (76%)
  local copies, waits for them, and re-layouts  4.28 us (11%)
  other arithmetic  3.93 us (10%)
  between operations  0.74 us (2%)
    pallas_call x1, Pallas kernels, attention(): pl.pallas_call(functools.partial(attention_kernel, lengths.shape[1], devi...  17.3 us
    pallas_call x1, Pallas kernels, finish(): pl.pallas_call(functools.partial(finish_kernel, peers, devices, width * p...  7.77 us
    pallas_call x1, Pallas kernels, token_scales(): pl.pallas_call(functools.partial(stat_kernel, peers), out_shape=jax.Shape...  5.25 us
    unnamed x20, local copies, waits for them, and re-layouts  3.56 us
    convert_element_type x1, other arithmetic, local(): (recip[0][:, None] * scaled_q - q_float * cubes[0][:, None]).astype(jnp.b...  2.05 us
    convert_element_type x1, other arithmetic, local(): (recip[1][:, None] * scaled_k - k_float * cubes[1][:, None]).astype(jnp.b...  1.22 us

profile of v5, /device:TPU:0, one launch (start us, length us, event | category | flops | bytes accessed | tf_op | source)
XLA Modules:
  0.0 39.3 jit_solution(4186176003398601546)
XLA Ops:
  0.6 0.0 copy-start.4
  0.6 0.0 copy-start.8
  0.7 0.0 copy-start.7
  0.7 0.0 copy-start.6
  0.7 0.7 %reshape.33.q_gain_ref = f32[1,640]{1,0:T(1,128)S(1)} reshape(f32[640]{0:T(1024)} %param.13) | data formatting | bytes 5120 | tf_op jit(solution)/shard_map/reshape | solution.py:436
  1.4 0.0 copy-start
  1.4 1.5 %copy-done = bf16[1536,640]{1,0:T(8,128)(2,1)S(1)} copy-done((bf16[1536,640]{1,0:T(8,128)(2,1)S(1)}, bf16[1536,640]{1,0:T(8,128)(2,1)}, u32[]{:S(2)}) %copy-start) | copy-done | bytes 1966104
  2.9 0.0 copy-start.2
  2.9 1.0 %copy-done.2 = bf16[1536,128]{1,0:T(8,128)(2,1)S(1)} copy-done((bf16[1536,128]{1,0:T(8,128)(2,1)S(1)}, bf16[1536,128]{1,0:T(8,128)(2,1)}, u32[]{:S(2)}) %copy-start.2) | copy-done | bytes 393240
  3.9 5.2 %shard_map.120.recip_ref = f32[24,128]{1,0:T(8,128)S(1)} custom-call(bf16[1536,640]{1,0:T(8,128)(2,1)S(1)} %copy-done, bf16[1536,128]{1,0:T(8,128)(2,1)S(1)} %copy-done.2), custom_call_target="tpu_custom_call" | custom-call | tf_op jit(solution)/shard_map/pallas_call | solution.py:314
  9.2 0.0 copy-done.4
  9.2 0.0 copy-done.8
  9.2 0.0 copy-done.7
  9.2 0.0 copy-done.6
  9.2 0.0 copy-done.1
  9.2 0.0 copy-done.3
  9.2 0.0 copy-start.5
  9.3 1.0 %copy-done.5 = bf16[1536,128]{1,0:T(8,128)(2,1)S(1)} copy-done((bf16[1536,128]{1,0:T(8,128)(2,1)S(1)}, bf16[1536,128]{1,0:T(8,128)(2,1)}, u32[]{:S(2)}) %copy-start.5) | copy-done | bytes 393240
  10.2 17.3 %shard_map.121 = (bf16[1536,640]{1,0:T(8,128)(2,1)S(1)}, bf16[1536,128]{1,0:T(8,128)(2,1)S(1)}, bf16[1536,128]{1,0:T(8,128)(2,1)}, f32[24,128]{1,0:T(8,128)S(1)}...) custom-call(s32[1,8]{1,0:T(1,128)S(1)} %copy-done.6, s32[1,8]{1,0:T(1,128)S(1)} %copy-done.7, s32[1,8]{1,0:T(1,128)S(1)} %copy-done.8, ...), custom_call_target="tpu_custom_call" | custom-call | flops 3774873600 | bytes 7864320 | tf_op jit(solution)/shard_map/pallas_call | solution.py:214
  27.6 7.8 %shard_map.122 = (f32[24,128]{1,0:T(8,128)S(1)}, f32[8,8,384]{2,1,0:T(8,128)S(1)}) custom-call(f32[24,128]{1,0:T(8,128)S(1)} %shard_map.120.recip_ref, f32[24,128]{1,0:T(8,128)S(1)} %get-tuple-element.13.back_ref, f32[8,8,384]{2,1,0:T(8,128)S(1)} %get-tuple-element.14.slots_ref), custom_call_target="tpu_custom_call" | custom-call | tf_op jit(solution)/shard_map/pallas_call | solution.py:399
  35.3 0.7 %pad_maximum_fusion = f32[5,3456]{1,0:T(8,128)} fusion(f32[5,3072]{1,0:T(8,128)S(1)} %bitcast.14, f32[5,384]{1,0:T(8,128)S(1)} %bitcast.15), kind=kLoop, calls=%fused_computation.2 | loop fusion | flops 17280 | bytes 138240 | tf_op jit(solution)/shard_map/concatenate | solution.py:446
  36.0 1.2 %subtract_convert_fusion.1 = bf16[1536,128]{1,0:T(8,128)(2,1)} fusion(bf16[1536,128]{1,0:T(8,128)(2,1)S(1)} %copy-done.3, bf16[1536,128]{1,0:T(8,128)(2,1)S(1)} %get-tuple-element.16, f32[1536]{0:T(1024)S(1)} %get-tuple-element.22, f32[128]{0:T(128)S(1)} %copy-done.4, f32[1536]{0:T(1024)S(1)} %get-tuple-element.25), kind=kLoop, calls=%fused_computation.1 | loop fusion | flops 1376256 | bytes 1192448 | tf_op jit(solution)/shard_map/convert_element_type | solution.py:454
  37.2 0.0 copy-done.9
  37.2 2.0 %subtract_convert_fusion = bf16[1536,640]{1,0:T(8,128)(2,1)} fusion(bf16[1536,640]{1,0:T(8,128)(2,1)S(1)} %copy-done.1, bf16[1536,640]{1,0:T(8,128)(2,1)S(1)} %get-tuple-element.12, f32[1536]{0:T(1024)S(1)} %get-tuple-element.23, f32[640]{0:T(1024)S(1)} %copy-done.9, f32[1536]{0:T(1024)S(1)} %get-tuple-element.24), kind=kLoop, calls=%fused_computation | loop fusion | flops 6881280 | bytes 5913088 | tf_op jit(solution)/shard_map/convert_element_type | solution.py:453
  (4 shorter events, 0.0 us)
Async XLA Ops:
  0.6 8.6 %copy-start.4 = (f32[128]{0:T(128)S(1)}, f32[128]{0:T(128)}, u32[]{:S(2)}) copy-start(f32[128]{0:T(128)} %param.14) | copy-start | bytes 1540
  0.6 8.6 %copy-start.8 = (s32[1,8]{1,0:T(1,128)S(1)}, s32[1,8]{1,0:T(1,128)}, u32[]{:S(2)}) copy-start(s32[1,8]{1,0:T(1,128)} %off_ref.1) | copy-start | bytes 100
  0.7 8.6 %copy-start.7 = (s32[1,8]{1,0:T(1,128)S(1)}, s32[1,8]{1,0:T(1,128)}, u32[]{:S(2)}) copy-start(s32[1,8]{1,0:T(1,128)} %dest_ref.1) | copy-start | bytes 100
  0.7 8.6 %copy-start.6 = (s32[1,8]{1,0:T(1,128)S(1)}, s32[1,8]{1,0:T(1,128)}, u32[]{:S(2)}) copy-start(s32[1,8]{1,0:T(1,128)} %len_ref.1) | copy-start | bytes 100
  1.4 1.5 %copy-start = (bf16[1536,640]{1,0:T(8,128)(2,1)S(1)}, bf16[1536,640]{1,0:T(8,128)(2,1)}, u32[]{:S(2)}) copy-start(bf16[1536,640]{1,0:T(8,128)(2,1)} %q_ref.3) | copy-start | bytes 5898244
  2.9 1.0 %copy-start.2 = (bf16[1536,128]{1,0:T(8,128)(2,1)S(1)}, bf16[1536,128]{1,0:T(8,128)(2,1)}, u32[]{:S(2)}) copy-start(bf16[1536,128]{1,0:T(8,128)(2,1)} %k_ref.3) | copy-start | bytes 1179652
  3.9 5.3 %copy-start.1 = (bf16[1536,640]{1,0:T(8,128)(2,1)S(1)}, bf16[1536,640]{1,0:T(8,128)(2,1)}, u32[]{:S(2)}) copy-start(bf16[1536,640]{1,0:T(8,128)(2,1)} %q_ref.3) | copy-start | bytes 5898244
  3.9 5.3 %copy-start.3 = (bf16[1536,128]{1,0:T(8,128)(2,1)S(1)}, bf16[1536,128]{1,0:T(8,128)(2,1)}, u32[]{:S(2)}) copy-start(bf16[1536,128]{1,0:T(8,128)(2,1)} %k_ref.3) | copy-start | bytes 1179652
  9.2 1.0 %copy-start.5 = (bf16[1536,128]{1,0:T(8,128)(2,1)S(1)}, bf16[1536,128]{1,0:T(8,128)(2,1)}, u32[]{:S(2)}) copy-start(bf16[1536,128]{1,0:T(8,128)(2,1)} %v_ref.1) | copy-start | bytes 1179652
  10.2 27.0 %copy-start.9 = (f32[640]{0:T(1024)S(1)}, f32[640]{0:T(1024)}, u32[]{:S(2)}) copy-start(f32[640]{0:T(1024)} %param.13) | copy-start | bytes 7684
